TPU v7x, 128 devices: a whole 4x4x4 slice. The times are simulated.
128 devices in a mesh: store: 4 (over z), trainer: 32 (over x, y, core).
Axes of the slice: x: 4, y: 4, z: 4, core: 2. Of those that a mesh axis runs over, the one named last changes fastest.
Arguments:
- features: bfloat16 [262144, 1024], P(('store', 'trainer')), may hold values from -6 to 6
- sent_ids: int32 [128, 32, 12], P(('store', 'trainer')), may hold values from 0 to 2047
- block_sizes: int32 [128, 32], P(('store', 'trainer')), may hold values from 1 to 12, as said below
- self_ids: int32 [24576], P('trainer'), may hold values from 0 to 1535, as said below
- near_one: int32 [24576, 10], P('trainer'), may hold values from 0 to 1535
- degree_one: int32 [24576], P('trainer'), may hold values from 1 to 10
- near_two: int32 [12288, 10], P('trainer'), may hold values from 0 to 767
- degree_two: int32 [12288], P('trainer'), may hold values from 1 to 10
- near_three: int32 [6144, 10], P('trainer'), may hold values from 0 to 383
- degree_three: int32 [6144], P('trainer'), may hold values from 1 to 10
- weight_one: bfloat16 [2048, 1024], P(None, 'store'), may hold values from -0.125 to 0.125
- weight_two: bfloat16 [2048, 1024], P(None, 'store'), may hold values from -0.125 to 0.125
- weight_three: bfloat16 [2048, 1024], P(None, 'store'), may hold values from -0.125 to 0.125
- cotangent: bfloat16 [6144, 1024], P('trainer', 'store'), may hold values from -6 to 6
Outputs:
- embedding: bfloat16 [6144, 1024], P('trainer', 'store')
- grad_one: float32 [2048, 1024], P('trainer', 'store')
- grad_two: float32 [2048, 1024], P('trainer', 'store')
- grad_three: float32 [2048, 1024], P('trainer', 'store')
Inputs may be any that keep to these rules, and one draw needn't show every extreme that they name: `block_sizes`: every owner sends 1 to 12 filled slots to every trainer group, and in every draw some trainer group receives exactly 12 filled slots from every owner. `self_ids`: each first-layer node names a filled slot: owner o = id // 12 and slot id % 12 < block_sizes[o, g] for its group g.
All inputs are finite; a program needn't handle non-finite values.
Results may differ from a plain program's by a relative error of at most 0.02.
Values may be sent and summed in bfloat16 or wider, within the bound.
A program may use at most 64 MiB of HBM per device.

v0:
```python
import jax
import jax.numpy as jnp
from jax import lax
from jax.sharding import PartitionSpec as P


def multiplicity(near, degree, width, filled):
    positions = lax.broadcasted_iota(jnp.int32, (near.shape[0], width), 1)
    total = jnp.zeros((near.shape[0], width), jnp.float32)
    for column in range(near.shape[1]):
        chosen = (near[:, column : column + 1] == positions) & (degree[:, None] > column)
        total = total + chosen.astype(jnp.float32)
    if filled is not None:
        total = total * filled[None, :]
    return (total.astype(jnp.bfloat16), 1.0 + jnp.sum(total, axis=1))


def average(below, own, tile, counted):
    summed = own.astype(jnp.float32) + jnp.dot(tile, below, preferred_element_type=jnp.float32)
    return (summed / counted[:, None]).astype(jnp.bfloat16)


def activate(preact):
    return (preact * jax.nn.sigmoid(preact)).astype(jnp.bfloat16)


def slope(preact):
    sigma = jax.nn.sigmoid(preact)
    return sigma * (1.0 + preact * (1.0 - sigma))


def deeper(hidden, near, degree):
    rows = near.shape[0]
    tile, counted = multiplicity(near, degree, hidden.shape[0], None)
    full_rows = lax.all_gather(hidden, "store", axis=1, tiled=True)
    own = full_rows[:rows]
    joined = jnp.concatenate([own, average(full_rows, own, tile, counted)], axis=1)
    return (joined, tile, counted)


def weight_grad(joined, dpre):
    return lax.psum_scatter(
        lax.dot_general(
            joined, dpre, (((0,), (0,)), ((), ())), preferred_element_type=jnp.float32
        ).astype(jnp.bfloat16),
        "trainer",
        scatter_dimension=0,
        tiled=True,
    ).astype(jnp.float32)


def back_step(dpre, weight, tile, counted, preact_below):
    rows = dpre.shape[0]
    spread = lax.dot_general(
        dpre, weight, (((1,), (1,)), ((), ())), preferred_element_type=jnp.float32
    )
    shares = lax.psum_scatter(spread.reshape(rows, 2, -1), "store", scatter_dimension=2, tiled=True)
    scaled = (shares[:, 1] / counted[:, None]).astype(jnp.bfloat16)
    below = lax.dot_general(
        tile, scaled, (((0,), (0,)), ((), ())), preferred_element_type=jnp.float32
    )
    upper = shares[:, 0] + scaled.astype(jnp.float32)
    below = below + jnp.pad(upper, ((0, below.shape[0] - rows), (0, 0)))
    return (below * slope(preact_below)).astype(jnp.bfloat16)


def shards(
    features,
    sent_ids,
    block_sizes,
    self_ids,
    near_one,
    degree_one,
    near_two,
    degree_two,
    near_three,
    degree_three,
    weight_one,
    weight_two,
    weight_three,
    cotangent,
):
    groups = lax.axis_size("trainer")
    stores = lax.axis_size("store")
    slots = sent_ids.shape[2]
    feature_width = features.shape[1]
    picked = jnp.take(features, sent_ids[0].reshape(-1), axis=0).reshape(
        groups, slots, feature_width
    )
    keeps = lax.broadcasted_iota(jnp.int32, (groups, slots), 1) < block_sizes[0][:, None]
    picked = jnp.where(keeps[:, :, None], picked, jnp.zeros((), jnp.bfloat16))
    sizes_wire = block_sizes[0].astype(jnp.bfloat16)[:, None]
    outgoing = jnp.tile(picked, (stores, 1, 1))
    counts_out = jnp.tile(sizes_wire, (stores, 1))
    arrived, arrived_counts = (
        lax.all_to_all(outgoing, ("store", "trainer"), split_axis=0, concat_axis=0, tiled=True),
        lax.all_to_all(counts_out, ("store", "trainer"), split_axis=0, concat_axis=0, tiled=True),
    )
    owners = arrived.shape[0]
    inputs = arrived.reshape(owners * slots, arrived.shape[2])
    slot_index = lax.broadcasted_iota(jnp.int32, (owners, slots), 1)
    filled = (slot_index < arrived_counts.astype(jnp.int32)).reshape(-1).astype(jnp.float32)
    own_one = jnp.take(inputs, self_ids, axis=0)
    tile_one, count_one = multiplicity(near_one, degree_one, inputs.shape[0], filled)
    joined_one = jnp.concatenate([own_one, average(inputs, own_one, tile_one, count_one)], axis=1)
    preact_one = jnp.dot(joined_one, weight_one, preferred_element_type=jnp.float32)
    hidden_one = activate(preact_one)
    joined_two, tile_two, count_two = deeper(hidden_one, near_two, degree_two)
    preact_two = jnp.dot(joined_two, weight_two, preferred_element_type=jnp.float32)
    hidden_two = activate(preact_two)
    joined_three, tile_three, count_three = deeper(hidden_two, near_three, degree_three)
    preact_three = jnp.dot(joined_three, weight_three, preferred_element_type=jnp.float32)
    embedding = preact_three.astype(jnp.bfloat16)
    grad_three = weight_grad(joined_three, cotangent)
    dpre_two = back_step(cotangent, weight_three, tile_three, count_three, preact_two)
    grad_two = weight_grad(joined_two, dpre_two)
    dpre_one = back_step(dpre_two, weight_two, tile_two, count_two, preact_one)
    grad_one = weight_grad(joined_one, dpre_one)
    return (embedding, grad_one, grad_two, grad_three)


def solution(mesh):
    placed = (
        P(("store", "trainer"), None),
        P(("store", "trainer"), None, None),
        P(("store", "trainer"), None),
        P("trainer"),
        P("trainer", None),
        P("trainer"),
        P("trainer", None),
        P("trainer"),
        P("trainer", None),
        P("trainer"),
        P(None, "store"),
        P(None, "store"),
        P(None, "store"),
        P("trainer", "store"),
    )
    return jax.shard_map(
        shards,
        mesh=mesh,
        in_specs=placed,
        out_specs=(
            P("trainer", "store"),
            P("trainer", "store"),
            P("trainer", "store"),
            P("trainer", "store"),
        ),
        check_vma=False,
    )
```

profile of v0, /device:TPU:3, one launch (start us, length us, event | category | flops | bytes accessed | tf_op | source)
XLA Modules:
  0.0 450.3 jit_solution(10492251872098939909)
XLA Ops:
  8.7 10.8 %all-to-all-start.1 = ((bf16[128,1,1]{2,1,0:T(2,128)(2,1)}), bf16[128,1,1]{2,1,0:T(2,128)(2,1)S(1)}, u32[]{:S(2)}, u32[]{:S(2)}) async-start(bf16[128,1,1]{2,1,0:T(2,128)(2,1)} %tile.21), calls=%async_computation.1 | async-start | bytes 131072 | tf_op jit(solution)/shard_map/all_to_all | solution.py:97
  22.0 5.5 %gather_fusion = bf16[384,1024]{1,0:T(8,128)(2,1)S(1)} fusion(bf16[2048,1024]{1,0:T(8,128)(2,1)} %param.14, s32[1024]{0:T(1024)S(1)} %pad_clamp_fusion.1), kind=kCustom, calls=%fused_computation | custom fusion | bytes 1574400 | tf_op jit(solution)/shard_map/jit(_take)/gather | solution.py:87
  28.0 2.5 tile.8
  30.5 10.1 %all-to-all-start = ((bf16[128,12,1024]{2,1,0:T(8,128)(2,1)}), bf16[128,12,1024]{2,1,0:T(8,128)(2,1)}, u32[]{:S(2)}, u32[]{:S(2)}) async-start(bf16[128,12,1024]{2,1,0:T(8,128)(2,1)} %bitcast.67), calls=%async_computation | async-start | bytes 8388608 | tf_op jit(solution)/shard_map/all_to_all | solution.py:96
  43.5 2.4 convert_reduce_fusion
  46.0 10.8 %fusion.32 = f32[768]{0:T(1024)S(1)} fusion(f32[1536]{0:T(1024)S(1)} %reshape.205, pred[768]{0:T(1024)(128)(4,1)S(1)} %get-tuple-element.42, s32[768]{0:T(1024)S(1)} %get-tuple-element.12, pred[768]{0:T(1024)(128)(4,1)S(1)} %get-tuple-element.43, s32[768]{0:T(1024)S(1)} %get-tuple-element.13, pred[768]{0:T(1024)(128)(4,1)S(1)} %get-tuple-element.35, ...), kind=kLoop, calls=%fused_computation.68 | loop fusion | flops 48364800 | bytes 47616 | tf_op jit(solution)/shard_map/reduce_sum | solution.py:15
  56.8 35.2 %all-to-all-done = bf16[128,12,1024]{2,1,0:T(8,128)(2,1)} async-done(((bf16[128,12,1024]{2,1,0:T(8,128)(2,1)}), bf16[128,12,1024]{2,1,0:T(8,128)(2,1)}, u32[]{:S(2)}, u32[]{:S(2)}) %all-to-all-start) | async-done | bytes 3145760 | tf_op jit(solution)/shard_map/all_to_all | solution.py:96
  92.0 6.2 %reshape.201 = bf16[1536,1024]{1,0:T(8,128)(2,1)} reshape(bf16[128,12,1024]{2,1,0:T(8,128)(2,1)} %all-to-all-done) | data formatting | bytes 6291456 | tf_op jit(solution)/shard_map/reshape | solution.py:100
  98.2 6.2 %gather_fusion.1 = bf16[768,1024]{1,0:T(8,128)(2,1)S(1)} fusion(bf16[1536,1024]{1,0:T(8,128)(2,1)} %reshape.201, s32[1024]{0:T(1024)S(1)} %pad_clamp_fusion), kind=kCustom, calls=%fused_computation.1 | custom fusion | bytes 3148800 | tf_op jit(solution)/shard_map/jit(_take)/gather | solution.py:103
  106.2 12.3 %divide_convert_fusion = bf16[768,1024]{1,0:T(8,128)(2,1)S(1)} fusion(bf16[768,1024]{1,0:T(8,128)(2,1)S(1)} %broadcast_select_fusion, bf16[1536,1024]{1,0:T(8,128)(2,1)S(1)} %copy-done.1, f32[768]{0:T(1024)S(1)} %broadcast_add_fusion, f32[1536]{0:T(1024)S(1)} %reshape.205, s32[768]{0:T(1024)S(1)} %get-tuple-element.12, s32[768]{0:T(1024)S(1)} %get-tuple-element.13, ...), kind=kOutput, calls=%fused_computation.24 | convolution fusion | flops 2467430400 | bytes 6339072 | tf_op jit(solution)/shard_map/dot_general | solution.py:19
  118.7 2.0 multiply_convert_fusion
  121.9 3.2 fusion.74
  126.3 22.0 %all-gather.2.cloned.1.call-done = bf16[768,1024]{1,0:T(8,128)(2,1)} async-done(((bf16[768,256]{1,0:T(8,128)(2,1)}), bf16[768,1024]{1,0:T(8,128)(2,1)}) %all-gather.2.cloned.1.call-update) | async-done | bytes 1572880 | tf_op jit(solution)/shard_map/all_gather | solution.py:35
  149.9 4.0 divide_convert_fusion.1
  155.7 2.4 fusion.77
  158.2 3.5 copy.41
  161.8 1.7 convolution_convert_fusion
  163.6 12.3 %all_gather.7 = bf16[384,1024]{1,0:T(8,128)(2,1)S(1)} all-gather(bf16[384,256]{1,0:T(8,128)(2,1)S(1)} %get-tuple-element.66), channel_id=1, replica_groups=mesh['store'=4,'trainer'=32] {'store'}, dimensions={1}, use_global_device_ids=true | all-gather | bytes 983040 | tf_op jit(solution)/shard_map/all_gather | solution.py:35
  179.2 24.2 %reduce-scatter.8.cloned.1.call-done = f32[384,2,256]{2,0,1:T(8,128)} async-done(((f32[384,2,1024]{2,0,1:T(8,128)}), f32[384,2,256]{2,0,1:T(8,128)}) %reduce-scatter.8.cloned.1.call-update) | async-done | bytes 786448 | tf_op jit(solution)/shard_map/reduce_scatter | solution.py:57
  204.8 2.8 fusion.17.clone.5
  207.7 2.1 convolution_convert_fusion.2
  210.8 70.6 %reduce-scatter.12.cloned.1.call-done = bf16[64,256]{1,0:T(8,128)(2,1)} async-done(((bf16[2048,256]{1,0:T(8,128)(2,1)}), bf16[64,256]{1,0:T(8,128)(2,1)}) %reduce-scatter.12.cloned.1.call-update) | async-done | bytes 32784 | tf_op jit(solution)/shard_map/reduce_scatter | solution.py:42
  282.8 79.2 %reduce-scatter.14.cloned.1.call-done = bf16[64,256]{1,0:T(8,128)(2,1)} async-done(((bf16[2048,256]{1,0:T(8,128)(2,1)}), bf16[64,256]{1,0:T(8,128)(2,1)}) %reduce-scatter.14.cloned.1.call-update) | async-done | bytes 32784 | tf_op jit(solution)/shard_map/reduce_scatter | solution.py:42
  363.3 78.8 %reduce-scatter.10.cloned.1.call-done = bf16[64,256]{1,0:T(8,128)(2,1)} async-done(((bf16[2048,256]{1,0:T(8,128)(2,1)}), bf16[64,256]{1,0:T(8,128)(2,1)}) %reduce-scatter.10.cloned.1.call-update) | async-done | bytes 32784 | tf_op jit(solution)/shard_map/reduce_scatter | solution.py:42
  (98 shorter events, 25.0 us)
Async XLA Ops:
  7.2 146.7 %copy-start = (bf16[2048,256]{1,0:T(8,128)(2,1)S(1)}, bf16[2048,256]{1,0:T(8,128)(2,1)}, u32[]{:S(2)}) copy-start(bf16[2048,256]{1,0:T(8,128)(2,1)} %param.25) | copy-start | bytes 3145732
  8.7 19.3 %all-to-all-start.1 = ((bf16[128,1,1]{2,1,0:T(2,128)(2,1)}), bf16[128,1,1]{2,1,0:T(2,128)(2,1)S(1)}, u32[]{:S(2)}, u32[]{:S(2)}) async-start(bf16[128,1,1]{2,1,0:T(2,128)(2,1)} %tile.21), calls=%async_computation.1 | async-start | bytes 131072 | tf_op jit(solution)/shard_map/all_to_all | solution.py:97
  30.5 10.2 %copy-start.4 = (bf16[2048,256]{1,0:T(8,128)(2,1)S(1)}, bf16[2048,256]{1,0:T(8,128)(2,1)}, u32[]{:S(2)}) copy-start(bf16[2048,256]{1,0:T(8,128)(2,1)} %param.26) | copy-start | bytes 3145732
  30.5 10.2 %copy-start.9 = (bf16[192,256]{1,0:T(8,128)(2,1)S(1)}, bf16[192,256]{1,0:T(8,128)(2,1)}, u32[]{:S(2)}) copy-start(bf16[192,256]{1,0:T(8,128)(2,1)} %param.27) | copy-start | bytes 294916
  30.5 61.5 %all-to-all-start = ((bf16[128,12,1024]{2,1,0:T(8,128)(2,1)}), bf16[128,12,1024]{2,1,0:T(8,128)(2,1)}, u32[]{:S(2)}, u32[]{:S(2)}) async-start(bf16[128,12,1024]{2,1,0:T(8,128)(2,1)} %bitcast.67), calls=%async_computation | async-start | bytes 8388608 | tf_op jit(solution)/shard_map/all_to_all | solution.py:96
  40.7 84.5 %reduce-scatter.6.cloned.1.call-start = ((), (), s32[]{:S(2)}) async-start(), calls=%async_computation.8 | async-start | bytes 1966080 | tf_op jit(solution)/shard_map/reduce_scatter | solution.py:57
  42.5 105.7 %all-gather.2.cloned.1.call-start = ((), (), s32[]{:S(2)}) async-start(), calls=%async_computation.7 | async-start | bytes 1966080 | tf_op jit(solution)/shard_map/all_gather | solution.py:35
  104.4 1.9 copy-start.1
  106.2 12.4 %copy-start.2 = (bf16[768,1024]{1,0:T(8,128)(2,1)}, bf16[768,1024]{1,0:T(8,128)(2,1)S(1)}, u32[]{:S(2)}) copy-start(bf16[768,1024]{1,0:T(8,128)(2,1)S(1)} %broadcast_select_fusion) | copy-start | bytes 4718596
  106.2 12.4 %copy-start.17 = (bf16[2048,256]{1,0:T(8,128)(2,1)S(1)}, bf16[2048,256]{1,0:T(8,128)(2,1)}, u32[]{:S(2)}) copy-start(bf16[2048,256]{1,0:T(8,128)(2,1)} %param.24) | copy-start | bytes 3145732
  118.6 2.1 copy-start.18
  118.6 2.4 copy-start.12
  118.6 2.4 copy-start.16
  118.7 2.5 copy-start.13
  118.7 3.2 copy-start.15
  120.7 82.7 %reduce-scatter.8.cloned.1.call-start = ((), (), s32[]{:S(2)}) async-start(), calls=%async_computation.9 | async-start | bytes 3932160 | tf_op jit(solution)/shard_map/reduce_scatter | solution.py:57
  148.2 1.6 copy-start.7
  161.8 119.6 %reduce-scatter.12.cloned.1.call-start = ((), (), s32[]{:S(2)}) async-start(), calls=%async_computation.11 | async-start | bytes 1081344 | tf_op jit(solution)/shard_map/reduce_scatter | solution.py:42
  163.6 198.4 %reduce-scatter.14.cloned.1.call-start = ((), (), s32[]{:S(2)}) async-start(), calls=%async_computation.12 | async-start | bytes 1081344 | tf_op jit(solution)/shard_map/reduce_scatter | solution.py:42
  179.1 25.6 %copy-start.20 = (f32[768,256]{1,0:T(8,128)S(1)}, f32[768,256]{1,0:T(8,128)}, u32[]{:S(2)}) copy-start(f32[768,256]{1,0:T(8,128)} %get-tuple-element.65) | copy-start | bytes 2359300
  179.2 262.9 %reduce-scatter.10.cloned.1.call-start = ((), (), s32[]{:S(2)}) async-start(), calls=%async_computation.10 | async-start | bytes 1081344 | tf_op jit(solution)/shard_map/reduce_scatter | solution.py:42
  204.8 2.8 copy-start.3
  204.8 2.8 copy-start.19
  207.6 2.1 copy-start.5
  (5 other events, 4.8 us)
Sparse Core Ops, SparseCore 0:
  43.9 58.2 reduce-scatter.5
  120.9 27.3 all-gather.1
  161.9 41.5 reduce-scatter.7
  206.8 74.5 reduce-scatter.11
  285.1 76.7 reduce-scatter.13
  365.3 76.7 reduce-scatter.9
where the time goes:
time: 454 us; the launch traced here: 450 us
  waiting for transfers between devices  310 us (68%)
  matrix products  33.6 us (7%)
  local copies, waits for them, and re-layouts  31.7 us (7%)
  other arithmetic  26.5 us (6%)
  starting transfers between devices  21.6 us (5%)
  between operations  14.5 us (3%)
  blocking collectives  12.3 us (3%)
    reduce_scatter x3, waiting for transfers between devices, weight_grad(): lax.psum_scatter(lax.dot_general(joined, dpre, (((0,), (0,)), ((), ())),...  229 us
    all_to_all x1, waiting for transfers between devices, shards(): lax.all_to_all(outgoing, ('store', 'trainer'), split_axis=0, concat_axis=...  35.2 us
    reduce_scatter x2, waiting for transfers between devices, back_step(): lax.psum_scatter(spread.reshape(rows, 2, -1), 'store', scatter_dimension=...  24.2 us
    all_gather x1, waiting for transfers between devices, deeper(): full_rows = lax.all_gather(hidden, 'store', axis=1, tiled=True)  22 us
    dot_general x3, matrix products, average(): jnp.dot(tile, below, preferred_element_type=jnp.float32)  18 us
    reduce_sum x3, other arithmetic, multiplicity(): return (total.astype(jnp.bfloat16), 1.0 + jnp.sum(total, axis=1))  14.7 us
    all_gather x1, blocking collectives, deeper(): full_rows = lax.all_gather(hidden, 'store', axis=1, tiled=True)  12.3 us
    all_to_all x1, starting transfers between devices, shards(): lax.all_to_all(counts_out, ('store', 'trainer'), split_axis=0, concat_axi...  10.8 us
  transfers between devices with their start and end apart: 8, of which 7 were waited for; matrix products, arithmetic and copies ran while one was open for 16% of the time, Pallas kernels for 0%

commit v1 on v0

v1 whole, which is shorter than its diff:
```python
import functools

import jax
import jax.numpy as jnp
from jax import lax
from jax.experimental import pallas as pl
from jax.experimental.pallas import tpu as pltpu
from jax.sharding import PartitionSpec as P

MESH = pl.DeviceIdType.MESH
F32 = jnp.float32
BF16 = jnp.bfloat16
SLOT = 16


def dot(a, b, left=1, right=0):
    return lax.dot_general(a, b, (((left,), (right,)), ((), ())), preferred_element_type=F32)


def slope(preact):
    sigma = jax.nn.sigmoid(preact)
    return sigma * (1.0 + preact * (1.0 - sigma))


def rows_at(index, size):
    return pl.ds(pl.multiple_of(index * size, size), size)


def step_of(rows, most):
    size = min(rows, most)
    while rows % size:
        size -= 1
    return size


def count_matches(ids, column_list, dst, rows, width):
    high = step_of(rows, 16)
    wide = step_of(width, 1024)

    def body(index, carry):
        part = ids[rows_at(index, high), :]
        for start in range(0, width, wide):
            place = lax.broadcasted_iota(jnp.int32, (high, wide), 1) + start
            total = jnp.zeros((high, wide), F32)
            for column in column_list:
                total = total + jnp.where(part[:, column : column + 1] == place, 1.0, 0.0)
            dst[rows_at(index, high), start : start + wide] = total.astype(BF16)
        return carry

    lax.fori_loop(0, rows // high, body, 0)


def kernel(
    stores, groups, slots,
    ids, near_one, near_two, near_three, cot, feat_hbm, one_hbm, two_hbm, three_hbm,
    emb_out, one_out, two_out, three_out,
    feat, hot, picked, arrived, filled, tile_one, tile_self, tile_two, tile_three,
    w_one, w_two, w_three, j_one, j_two, j_three, pre_one, pre_two, hid_one, hid_two,
    sp3_send, sp3_recv, sp2_send, sp2_recv, below3, dpre_two, dpre_one, full,
    px_send, px_recv, blk, rr,
    load_sem, in_send, in_recv,
    ag1_send, ag1_recv, ag2_send, ag2_recv, ag3_send, ag3_recv,
    sp_send_sem, sp_recv_sem, px_ssem, px_rsem, rr_ssem, rr_rsem,
):
    devices = stores * groups
    z = lax.axis_index("store")
    t = lax.axis_index("trainer")
    me = z * groups + t
    chip, core = t // 2, lax.rem(t, 2)
    chips = groups // 2
    right, left, across = (lax.rem(z + k, stores) for k in (1, 3, 2))
    width = cot.shape[1]
    seeds, mid, outer = cot.shape[0], near_two.shape[0], near_one.shape[0]
    cells = devices * SLOT

    def remote(src, dst, send_sem, recv_sem, store, trainer):
        return pltpu.make_async_remote_copy(
            src_ref=src, dst_ref=dst, send_sem=send_sem, recv_sem=recv_sem,
            device_id=(store, trainer), device_id_type=MESH,
        )

    def await_bytes(ref, sem):
        pltpu.make_async_copy(ref, ref, sem).wait()

    barrier = pltpu.get_barrier_semaphore()

    def greet(index, carry):
        other = lax.rem(me + index, devices)
        pl.semaphore_signal(
            barrier, inc=1, device_id=(other // groups, lax.rem(other, groups)), device_id_type=MESH
        )
        return carry

    lax.fori_loop(1, devices, greet, 0)

    loads = [pltpu.make_async_copy(feat_hbm, feat, load_sem.at[0])]
    for place, (hbm, held) in enumerate(((one_hbm, w_one), (two_hbm, w_two), (three_hbm, w_three))):
        for store in range(stores):
            for half in range(2):
                source = half * stores * width + store * width
                loads.append(
                    pltpu.make_async_copy(
                        hbm.at[pl.ds(source, width), :],
                        held.at[store, pl.ds(half * width, width), :],
                        load_sem.at[1 + (place * stores + store) * 2 + half],
                    )
                )
    for load in loads:
        load.start()

    count_matches(ids, [0], hot, groups * SLOT, feat.shape[0])
    loads[0].wait()
    pl.semaphore_wait(barrier, devices - 1)

    def fetch(index, carry):
        store = lax.rem(z + index, stores)
        columns = pl.ds(pl.multiple_of(store * width, width), width)
        rows = step_of(groups * SLOT, 256)
        for start in range(0, groups * SLOT, rows):
            part = dot(hot[start : start + rows, :], feat[:, columns])
            counts = ids[start : start + rows, 1:2].astype(F32)
            picked[store, start : start + rows, :] = (part + counts).astype(BF16)

        def send(number, inner):
            trainer = lax.rem(t + number * 13, groups)

            @pl.when(jnp.logical_or(store != z, trainer != t))
            def _():
                remote(
                    picked.at[store, rows_at(trainer, SLOT), :], arrived.at[rows_at(me, SLOT), :],
                    in_send.at[store], in_recv.at[z], store, trainer,
                ).start()

            return inner

        lax.fori_loop(0, groups, send, 0)
        return carry

    lax.fori_loop(0, stores, fetch, 0)
    own_block = pltpu.make_async_copy(
        picked.at[z, rows_at(t, SLOT), :], arrived.at[rows_at(me, SLOT), :], in_recv.at[z]
    )
    own_block.start()
    for load in loads[1:]:
        load.wait()

    others = ((right, 0), (left, 1), (across, 2))

    def send_spread(dpre, weight, send, recv, number):
        for store, place in others:
            send[place] = dot(dpre[...], weight[store], 1, 1).astype(BF16)
            remote(
                send.at[place], recv.at[place],
                sp_send_sem.at[number, place], sp_recv_sem.at[number, place], store, t,
            ).start()

    def take_spread(dpre, weight, recv, number):
        total = dot(dpre[...], weight[z], 1, 1)
        for place in range(3):
            await_bytes(recv.at[place], sp_recv_sem.at[number, place])
            total = total + recv[place].astype(F32)
        return total

    send_spread(cot, w_three, sp3_send, sp3_recv, 0)

    fan = near_two.shape[1]
    count_matches(near_one, list(range(fan)), tile_one, outer, cells)
    count_matches(near_one, [fan], tile_self, outer, cells)
    count_matches(near_two, list(range(fan)), tile_two, mid, outer)
    count_matches(near_three, list(range(fan)), tile_three, seeds, mid)

    def counted(near):
        return 1.0 + jnp.sum(jnp.where(near[...] >= 0, 1.0, 0.0), axis=1, keepdims=True)

    def spread_below(total, near, tile, below_rows):
        rows = near.shape[0]
        scaled = (total[:, width:] / counted(near)).astype(BF16)
        below = dot(tile[...], scaled, 0, 0)
        upper = below[:rows] + (total[:, :width] + scaled.astype(F32))
        return jnp.concatenate([upper, below[rows:]], axis=0)

    below3[...] = spread_below(take_spread(cot, w_three, sp3_recv, 0), near_three, tile_three, mid)

    def start_gather(held, index, rows, send_sem, recv_sem):
        piece = held.at[z, rows_at(index, rows), :]
        remote(piece, piece, send_sem.at[0, index], recv_sem.at[0, index], right, t).start()
        remote(piece, piece, send_sem.at[1, index], recv_sem.at[1, index], left, t).start()

    def take_gather(held, chunks, rows, send_sem, recv_sem, use):
        for index in range(chunks):
            here = rows_at(index, rows)
            for side, (source, onward) in enumerate(((left, right), (right, left))):
                piece = held.at[source, here, :]
                await_bytes(piece, recv_sem.at[side, index])
                if index % 2 == side:
                    remote(piece, piece, send_sem.at[2, index], recv_sem.at[2, index], onward, t).start()
            for source in (left, right):
                use(source, here)
        for index in range(chunks):
            here = rows_at(index, rows)
            await_bytes(held.at[across, here, :], recv_sem.at[2, index])
            use(across, here)

    def finish_gather(held, chunks, rows, send_sem):
        for way in range(3):
            for index in range(chunks):
                await_bytes(held.at[z, rows_at(index, rows), :], send_sem.at[way, index])

    for store in range(stores):
        await_bytes(arrived.at[pl.ds(store * groups * SLOT, groups * SLOT), :], in_recv.at[store])

    def mark(index, carry):
        here = rows_at(index, SLOT)
        block = arrived[here, 0 : filled.shape[1]].astype(F32)
        place = lax.broadcasted_iota(jnp.int32, block.shape, 0).astype(F32)
        filled[here, :] = jnp.where(place < block[slots : slots + 1, :], 1.0, 0.0).astype(BF16)
        return carry

    lax.fori_loop(0, devices, mark, 0)

    chunks_one = ag1_send.shape[1]
    rows_one = outer // chunks_one

    def layer_one(index, carry):
        here = rows_at(index, rows_one)
        own = dot(tile_self[here, :], arrived[...])
        valid = 1.0 + dot(tile_one[here, :], filled[...])
        valid = jnp.concatenate([valid] * (width // valid.shape[1]), axis=1)
        mean = (own + dot(tile_one[here, :], arrived[...])) / valid
        j_one[z, here, :] = jnp.concatenate([own, mean], axis=1).astype(BF16)
        start_gather(j_one, index, rows_one, ag1_send, ag1_recv)
        pre_one[here, :] = dot(j_one[z, here, :], w_one[z])
        return carry

    lax.fori_loop(0, chunks_one, layer_one, 0)

    def use_one(source, here):
        pre_one[here, :] += dot(j_one[source, here, :], w_one[source])

    take_gather(j_one, chunks_one, rows_one, ag1_send, ag1_recv, use_one)
    hid_one[...] = (pre_one[...] * jax.nn.sigmoid(pre_one[...])).astype(BF16)

    def join(hidden, near, tile, joined, chunks, send_sem, recv_sem):
        rows = near.shape[0]
        own = hidden[0:rows, :]
        mean = (own.astype(F32) + dot(tile[...], hidden[...])) / counted(near)
        joined[z] = jnp.concatenate([own, mean.astype(BF16)], axis=1)
        for index in range(chunks):
            start_gather(joined, index, rows // chunks, send_sem, recv_sem)

    chunks_two, chunks_three = ag2_send.shape[1], ag3_send.shape[1]
    rows_two, rows_three = mid // chunks_two, seeds // chunks_three
    join(hid_one, near_two, tile_two, j_two, chunks_two, ag2_send, ag2_recv)
    pre_two[...] = dot(j_two[z], w_two[z])

    def use_two(source, here):
        pre_two[here, :] += dot(j_two[source, here, :], w_two[source])

    take_gather(j_two, chunks_two, rows_two, ag2_send, ag2_recv, use_two)
    dpre_two[...] = (below3[...] * slope(pre_two[...])).astype(BF16)
    send_spread(dpre_two, w_two, sp2_send, sp2_recv, 1)
    hid_two[...] = (pre_two[...] * jax.nn.sigmoid(pre_two[...])).astype(BF16)
    join(hid_two, near_three, tile_three, j_three, chunks_three, ag3_send, ag3_recv)

    height = full.shape[1]
    per_slice = width // height

    def start_grad(number, joined, dpre):
        def products(store, carry):
            part = dot(joined[store], dpre[...], 0, 0)
            for half in range(2):
                for index in range(per_slice):
                    start = half * width + index * height
                    full[half * (groups // 2) + store * per_slice + index] = part[start : start + height, :]
            return carry

        lax.fori_loop(0, stores, products, 0)

        def pack(index, carry):
            px_send[number, index] = full[index * 2 + 1 - core].astype(BF16)
            return carry

        lax.fori_loop(0, chips, pack, 0)
        remote(
            px_send.at[number], px_recv.at[number], px_ssem.at[number], px_rsem.at[number], z, t + 1 - 2 * core
        ).start()
        await_bytes(px_recv.at[number], px_rsem.at[number])

        def spread(index, carry):
            target = lax.rem(chip + index, chips)
            total = full[target * 2 + core] + px_recv[number, target].astype(F32)
            blk[number, target] = total.astype(BF16)

            @pl.when(index > 0)
            def _():
                remote(
                    blk.at[number, target], rr.at[number, chip],
                    rr_ssem.at[number], rr_rsem.at[number], z, target * 2 + core,
                ).start()

            @pl.when(index == 0)
            def _():
                rr[number, chip] = total.astype(BF16)

            return carry

        lax.fori_loop(0, chips, spread, 0)

    def finish_grad(number, out):
        await_bytes(rr.at[number, pl.ds(0, chips - 1)], rr_rsem.at[number])
        out[...] = jnp.sum(rr[number].astype(F32), axis=0)

    start_grad(1, j_two, dpre_two)
    below2 = spread_below(take_spread(dpre_two, w_two, sp2_recv, 1), near_two, tile_two, outer)
    dpre_one[...] = (below2 * slope(pre_one[...])).astype(BF16)
    start_grad(0, j_one, dpre_one)

    emb = [dot(j_three[z], w_three[z])]

    def use_three(source, here):
        emb[0] = emb[0] + dot(j_three[source], w_three[source])

    def keep(source, here):
        return None

    take_gather(j_three, chunks_three, rows_three, ag3_send, ag3_recv, keep)
    for source in (left, right, across):
        use_three(source, None)
    emb_out[...] = emb[0].astype(BF16)
    start_grad(2, j_three, cot)

    finish_grad(1, two_out)
    finish_grad(0, one_out)
    finish_grad(2, three_out)

    for index in range(stores):
        store = lax.rem(z + index, stores)
        amount = groups - (1 if index == 0 else 0)
        await_bytes(picked.at[store, pl.ds(0, amount * SLOT), :], in_send.at[store])
    finish_gather(j_one, chunks_one, rows_one, ag1_send)
    finish_gather(j_two, chunks_two, rows_two, ag2_send)
    finish_gather(j_three, chunks_three, rows_three, ag3_send)
    for place in range(3):
        await_bytes(sp3_send.at[place], sp_send_sem.at[0, place])
        await_bytes(sp2_send.at[place], sp_send_sem.at[1, place])
    for number in range(3):
        await_bytes(px_send.at[number], px_ssem.at[number])
        await_bytes(blk.at[number, pl.ds(0, chips - 1)], rr_ssem.at[number])


def run(
    stores, groups, features, sent_ids, block_sizes, self_ids, near_one, degree_one, near_two, degree_two,
    near_three, degree_three, weight_one, weight_two, weight_three, cotangent,
):
    slots = sent_ids.shape[2]
    outer, mid, seeds = near_one.shape[0], near_two.shape[0], near_three.shape[0]
    fan = near_one.shape[1]
    fwidth = features.shape[1]
    width = cotangent.shape[1]
    devices = stores * groups
    cells = devices * SLOT
    height = 2 * fwidth // groups

    place = lax.broadcasted_iota(jnp.int32, (groups, SLOT), 1)
    sizes = block_sizes[0][:, None]
    padded = jnp.pad(sent_ids[0], ((0, 0), (0, SLOT - slots)))
    ids = jnp.stack(
        [jnp.where(place < sizes, padded, -1), jnp.where(place == slots, sizes, 0)], axis=-1
    ).reshape(groups * SLOT, 2)

    def used(near, degree):
        column = lax.broadcasted_iota(jnp.int32, near.shape, 1)
        return jnp.where(column < degree[:, None], near, -1)

    def moved(index):
        return index // slots * SLOT + lax.rem(index, slots)

    ids_one = jnp.concatenate([used(moved(near_one), degree_one), moved(self_ids)[:, None]], axis=1)
    vmem = pl.BlockSpec(memory_space=pltpu.VMEM)
    hbm = pl.BlockSpec(memory_space=pl.ANY)
    lanes = min(128, width)
    c1, c2, c3 = 4, 2, 2
    dma = pltpu.SemaphoreType.DMA
    chips = groups // 2
    scratch = [
        pltpu.VMEM(features.shape, BF16),
        pltpu.VMEM((groups * SLOT, features.shape[0]), BF16),
        pltpu.VMEM((stores, groups * SLOT, width), BF16),
        pltpu.VMEM((cells, width), BF16),
        pltpu.VMEM((cells, lanes), BF16),
        pltpu.VMEM((outer, cells), BF16),
        pltpu.VMEM((outer, cells), BF16),
        pltpu.VMEM((mid, outer), BF16),
        pltpu.VMEM((seeds, mid), BF16),
    ]
    scratch += [pltpu.VMEM((stores, 2 * width, width), BF16)] * 3
    scratch += [pltpu.VMEM((stores, rows, 2 * width), BF16) for rows in (outer, mid, seeds)]
    scratch += [pltpu.VMEM((rows, width), F32) for rows in (outer, mid)]
    scratch += [pltpu.VMEM((rows, width), BF16) for rows in (outer, mid)]
    scratch += [pltpu.VMEM((3, seeds, 2 * width), BF16)] * 2 + [pltpu.VMEM((3, mid, 2 * width), BF16)] * 2
    scratch += [
        pltpu.VMEM((mid, width), F32),
        pltpu.VMEM((mid, width), BF16),
        pltpu.VMEM((outer, width), BF16),
        pltpu.VMEM((groups, height, width), F32),
    ]
    scratch += [pltpu.VMEM((3, chips, height, width), BF16)] * 4
    scratch += [dma((1 + 6 * stores,)), dma((stores,)), dma((stores,))]
    scratch += [dma((3, chunks)) for chunks in (c1, c1, c2, c2, c3, c3)]
    scratch += [dma((2, 3)), dma((2, 3)), dma((3,)), dma((3,)), dma((3,)), dma((3,))]
    return pl.pallas_call(
        functools.partial(kernel, stores, groups, slots),
        out_shape=(
            jax.ShapeDtypeStruct((seeds, width), BF16),
            jax.ShapeDtypeStruct((height, width), F32),
            jax.ShapeDtypeStruct((height, width), F32),
            jax.ShapeDtypeStruct((height, width), F32),
        ),
        in_specs=[vmem] * 5 + [hbm] * 4,
        out_specs=(vmem,) * 4,
        scratch_shapes=scratch,
        compiler_params=pltpu.CompilerParams(
            collective_id=0, has_side_effects=True, vmem_limit_bytes=60 * 1024 * 1024
        ),
    )(
        ids, ids_one, used(near_two, degree_two), used(near_three, degree_three), cotangent,
        features, weight_one, weight_two, weight_three,
    )


def solution(mesh):
    stores, groups = mesh.shape["store"], mesh.shape["trainer"]
    both = ("store", "trainer")
    placed = (
        P(both, None), P(both, None, None), P(both, None), P("trainer"), P("trainer", None), P("trainer"),
        P("trainer", None), P("trainer"), P("trainer", None), P("trainer"),
        P(None, "store"), P(None, "store"), P(None, "store"), P("trainer", "store"),
    )
    return jax.shard_map(
        functools.partial(run, stores, groups),
        mesh=mesh, in_specs=placed, out_specs=(P("trainer", "store"),) * 4, check_vma=False,
    )
```

time: 454 us -> 143 us (0.31)
  waiting for transfers between devices: 310 us -> 0 us
  Pallas kernels: 0 us -> 124 us
  matrix products: 33.6 us -> 0 us
  starting transfers between devices: 21.6 us -> 0 us
  other arithmetic: 26.5 us -> 5.14 us
  local copies, waits for them, and re-layouts: 31.7 us -> 11.2 us
  between operations: 14.5 us -> 0.69 us
  blocking collectives: 12.3 us -> 0 us
    reduce_scatter x5 -> x0, waiting for transfers between devices: 253 us -> none  [the longest x3 229 us: weight_grad(): lax.psum_scatter(lax.dot_general(joined, dpre, (((0,), (0,)), ((), ())),...]
    pallas_call x0 -> x1, Pallas kernels: none -> 124 us  [run(): pl.pallas_call(functools.partial(kernel, stores, groups, slots), out_shap...]
    all_to_all x2 -> x0, waiting for transfers between devices: 35.3 us -> none  [the longest x1 35.2 us: shards(): lax.all_to_all(outgoing, ('store', 'trainer'), split_axis=0, concat_axis=...]
    dot_general x13 -> x0, matrix products: 33.6 us -> none  [the longest x3 18 us: average(): jnp.dot(tile, below, preferred_element_type=jnp.float32)]
    all_gather x1 -> x0, waiting for transfers between devices: 22 us -> none  [deeper(): full_rows = lax.all_gather(hidden, 'store', axis=1, tiled=True)]
    all_to_all x2 -> x0, starting transfers between devices: 21 us -> none  [the longest x1 10.8 us: shards(): lax.all_to_all(counts_out, ('store', 'trainer'), split_axis=0, concat_axi...]
    reduce_sum x3 -> x0, other arithmetic: 14.7 us -> none  [multiplicity(): return (total.astype(jnp.bfloat16), 1.0 + jnp.sum(total, axis=1))]
    all_gather x1 -> x0, blocking collectives: 12.3 us -> none  [deeper(): full_rows = lax.all_gather(hidden, 'store', axis=1, tiled=True)]
  transfers between devices with their start and end apart: 8 -> 0, of which waited for: 7 -> 0; matrix products, arithmetic and copies ran while one was open for 16% -> 0% of each run, Pallas kernels for 0% -> 0%
where the time goes in v1:
time: 143 us; the launch traced here: 141 us
  Pallas kernels  124 us (87%)
  local copies, waits for them, and re-layouts  11.2 us (8%)
  other arithmetic  5.14 us (4%)
    pallas_call x1, Pallas kernels, run(): pl.pallas_call(functools.partial(kernel, stores, groups, slots), out_shap...  124 us
    unnamed x7, local copies, waits for them, and re-layouts  8.34 us
    select_n x3, other arithmetic, used(): return jnp.where(column < degree[:, None], near, -1)  3.74 us

profile of v1, /device:TPU:3, one launch (start us, length us, event | category | flops | bytes accessed | tf_op | source)
XLA Modules:
  0.0 140.8 jit_solution(2720409750270469344)
XLA Ops:
  0.7 0.1 iota.29
  0.7 0.7 fusion.7
  1.5 0.7 copy.44
  2.2 0.7 pad_select_fusion
  2.8 0.1 copy.36
  2.9 0.1 stack.7
  3.0 0.7 lt.37.clone
  3.7 0.1 lt.39
  3.8 0.8 fusion.4
  4.7 0.8 copy.39
  5.5 1.4 %fusion.1.near_three = s32[192,10]{1,0:T(8,128)} fusion(s32[192,10]{1,0:T(8,128)S(1)} %copy.39, s32[192]{0:T(256)} %param.23), kind=kLoop, calls=%fused_computation.3 | loop fusion | flops 3840 | bytes 16128 | tf_op jit(solution)/shard_map/jit(_where)/select_n | solution.py:373
  6.9 0.9 copy.38
  7.8 1.5 %fusion.near_two = s32[384,10]{1,0:T(8,128)} fusion(s32[384,10]{1,0:T(8,128)S(1)} %copy.38, s32[384]{0:T(512)} %param.21), kind=kLoop, calls=%fused_computation.1 | loop fusion | flops 7680 | bytes 32256 | tf_op jit(solution)/shard_map/jit(_where)/select_n | solution.py:373
  9.3 0.9 copy.40.ids
  10.1 0.9 copy.41.near_one
  11.1 123.8 %shard_map.165 = (bf16[192,256]{1,0:T(8,128)(2,1)}, f32[64,256]{1,0:T(8,128)}, f32[64,256]{1,0:T(8,128)}, f32[64,256]{1,0:T(8,128)}) custom-call(s32[512,2]{1,0:T(8,128)} %copy.40.ids, s32[768,11]{1,0:T(8,128)} %copy.41.near_one, s32[384,10]{1,0:T(8,128)} %fusion.near_two, s32[192,10]{1,0:T(8,128)} %fusion.1.near_three, bf16[192,256]{1,0:T(8,128)(2,1)} %cot.1, ...), custom_call_target="tpu_custom_call" | custom-call | tf_op jit(solution)/shard_map/pallas_call | solution.py:411
  134.9 1.5 %copy.49 = bf16[192,256]{1,0:T(8,128)(2,1)} copy(bf16[192,256]{1,0:T(8,128)(2,1)} %get-tuple-element.8) | data formatting | bytes 196608
  136.4 1.5 %copy.50 = f32[64,256]{1,0:T(8,128)} copy(f32[64,256]{1,0:T(8,128)} %get-tuple-element.9) | data formatting | bytes 131072
  137.9 1.5 %copy.51 = f32[64,256]{1,0:T(8,128)} copy(f32[64,256]{1,0:T(8,128)} %get-tuple-element.10) | data formatting | bytes 131072
  139.3 1.5 %copy.52 = f32[64,256]{1,0:T(8,128)} copy(f32[64,256]{1,0:T(8,128)} %get-tuple-element.11) | data formatting | bytes 131072
  (6 shorter events, 0.0 us)

commit v2 on v1

--- a/solution.py
+++ b/solution.py
@@ -52,9 +52,10 @@
 
 def kernel(
     stores, groups, slots,
-    ids, near_one, near_two, near_three, cot, feat_hbm, one_hbm, two_hbm, three_hbm,
+    sent, sizes, self_ids, near_one_t, degree_one, near_two_t, degree_two, near_three_t, degree_three,
+    cot, feat_hbm, one_hbm, two_hbm, three_hbm,
     emb_out, one_out, two_out, three_out,
-    feat, hot, picked, arrived, filled, tile_one, tile_self, tile_two, tile_three,
+    near_one, near_two, near_three, extra, feat, hot, picked, arrived, filled, tile_one, tile_self, tile_two, tile_three,
     w_one, w_two, w_three, j_one, j_two, j_three, pre_one, pre_two, hid_one, hid_two,
     sp3_send, sp3_recv, sp2_send, sp2_recv, below3, dpre_two, dpre_one, full,
     px_send, px_recv, blk, rr,
@@ -72,6 +73,7 @@
     width = cot.shape[1]
     seeds, mid, outer = cot.shape[0], near_two.shape[0], near_one.shape[0]
     cells = devices * SLOT
+    pending = []
 
     def remote(src, dst, send_sem, recv_sem, store, trainer):
         return pltpu.make_async_remote_copy(
@@ -108,7 +110,18 @@
     for load in loads:
         load.start()
 
-    count_matches(ids, [0], hot, groups * SLOT, feat.shape[0])
+    slot = lax.broadcasted_iota(jnp.int32, (SLOT, groups), 0)
+    amounts = jnp.broadcast_to(sizes[...], (SLOT, groups))
+    wanted = jnp.concatenate([sent[index] for index in range(slots)] + [jnp.full((SLOT - slots, groups), -1, jnp.int32)], axis=0)
+    wanted = jnp.where(slot < amounts, wanted, -1)
+    notes = jnp.where(slot == slots, amounts, 0).astype(F32)
+    wide = step_of(feat.shape[0], 1024)
+    for group in range(groups):
+        here = pl.ds(group * SLOT, SLOT)
+        extra[here, :] = jnp.broadcast_to(notes[:, group : group + 1], (SLOT, extra.shape[1]))
+        for start in range(0, feat.shape[0], wide):
+            place = lax.broadcasted_iota(jnp.int32, (SLOT, wide), 1) + start
+            hot[here, start : start + wide] = jnp.where(wanted[:, group : group + 1] == place, 1.0, 0.0).astype(BF16)
     loads[0].wait()
     pl.semaphore_wait(barrier, devices - 1)
 
@@ -118,7 +131,7 @@
         rows = step_of(groups * SLOT, 256)
         for start in range(0, groups * SLOT, rows):
             part = dot(hot[start : start + rows, :], feat[:, columns])
-            counts = ids[start : start + rows, 1:2].astype(F32)
+            counts = jnp.concatenate([extra[start : start + rows, :]] * (width // extra.shape[1]), axis=1)
             picked[store, start : start + rows, :] = (part + counts).astype(BF16)
 
         def send(number, inner):
@@ -141,6 +154,14 @@
         picked.at[z, rows_at(t, SLOT), :], arrived.at[rows_at(me, SLOT), :], in_recv.at[z]
     )
     own_block.start()
+
+    def leave_blocks():
+        for index in range(stores):
+            store = lax.rem(z + index, stores)
+            amount = groups - (1 if index == 0 else 0)
+            await_bytes(picked.at[store, pl.ds(0, amount * SLOT), :], in_send.at[store])
+
+    pending.append(leave_blocks)
     for load in loads[1:]:
         load.wait()
 
@@ -153,6 +174,7 @@
                 send.at[place], recv.at[place],
                 sp_send_sem.at[number, place], sp_recv_sem.at[number, place], store, t,
             ).start()
+            pending.append(lambda place=place: await_bytes(send.at[place], sp_send_sem.at[number, place]))
 
     def take_spread(dpre, weight, recv, number):
         total = dot(dpre[...], weight[z], 1, 1)
@@ -163,7 +185,21 @@
 
     send_spread(cot, w_three, sp3_send, sp3_recv, 0)
 
-    fan = near_two.shape[1]
+    fan = near_two_t.shape[0]
+
+    def moved(index):
+        return index + (SLOT - slots) * ((index * ((1 << 19) // slots + 1)) >> 19)
+
+    def upright(near, degree, own, dst):
+        rows = near.shape[1]
+        place = lax.broadcasted_iota(jnp.int32, (fan, rows), 0)
+        parts = [jnp.where(place < degree[...][None, :], near, -1)] + own
+        parts.append(jnp.full((SLOT - fan - len(own), rows), -1, jnp.int32))
+        dst[...] = jnp.concatenate(parts, axis=0).T
+
+    upright(moved(near_one_t[...]), degree_one, [moved(self_ids[...][None, :])], near_one)
+    upright(near_two_t[...], degree_two, [], near_two)
+    upright(near_three_t[...], degree_three, [], near_three)
     count_matches(near_one, list(range(fan)), tile_one, outer, cells)
     count_matches(near_one, [fan], tile_self, outer, cells)
     count_matches(near_two, list(range(fan)), tile_two, mid, outer)
@@ -200,11 +236,13 @@
             here = rows_at(index, rows)
             await_bytes(held.at[across, here, :], recv_sem.at[2, index])
             use(across, here)
-
-    def finish_gather(held, chunks, rows, send_sem):
         for way in range(3):
             for index in range(chunks):
-                await_bytes(held.at[z, rows_at(index, rows), :], send_sem.at[way, index])
+                pending.append(
+                    lambda way=way, here=rows_at(index, rows), index=index: await_bytes(
+                        held.at[z, here, :], send_sem.at[way, index]
+                    )
+                )
 
     for store in range(stores):
         await_bytes(arrived.at[pl.ds(store * groups * SLOT, groups * SLOT), :], in_recv.at[store])
@@ -284,6 +322,7 @@
         remote(
             px_send.at[number], px_recv.at[number], px_ssem.at[number], px_rsem.at[number], z, t + 1 - 2 * core
         ).start()
+        pending.append(lambda: await_bytes(px_send.at[number], px_ssem.at[number]))
         await_bytes(px_recv.at[number], px_rsem.at[number])
 
         def spread(index, carry):
@@ -305,6 +344,7 @@
             return carry
 
         lax.fori_loop(0, chips, spread, 0)
+        pending.append(lambda: await_bytes(blk.at[number, pl.ds(0, chips - 1)], rr_ssem.at[number]))
 
     def finish_grad(number, out):
         await_bytes(rr.at[number, pl.ds(0, chips - 1)], rr_rsem.at[number])
@@ -333,19 +373,14 @@
     finish_grad(0, one_out)
     finish_grad(2, three_out)
 
-    for index in range(stores):
-        store = lax.rem(z + index, stores)
-        amount = groups - (1 if index == 0 else 0)
-        await_bytes(picked.at[store, pl.ds(0, amount * SLOT), :], in_send.at[store])
-    finish_gather(j_one, chunks_one, rows_one, ag1_send)
-    finish_gather(j_two, chunks_two, rows_two, ag2_send)
-    finish_gather(j_three, chunks_three, rows_three, ag3_send)
-    for place in range(3):
-        await_bytes(sp3_send.at[place], sp_send_sem.at[0, place])
-        await_bytes(sp2_send.at[place], sp_send_sem.at[1, place])
-    for number in range(3):
-        await_bytes(px_send.at[number], px_ssem.at[number])
-        await_bytes(blk.at[number, pl.ds(0, chips - 1)], rr_ssem.at[number])
+    for leave in pending:
+        leave()
+
+
+def copies(*refs):
+    half = len(refs) // 2
+    for source, target in zip(refs[:half], refs[half:]):
+        target[...] = source[...]
 
 
 def run(
@@ -361,28 +396,15 @@
     cells = devices * SLOT
     height = 2 * fwidth // groups
 
-    place = lax.broadcasted_iota(jnp.int32, (groups, SLOT), 1)
-    sizes = block_sizes[0][:, None]
-    padded = jnp.pad(sent_ids[0], ((0, 0), (0, SLOT - slots)))
-    ids = jnp.stack(
-        [jnp.where(place < sizes, padded, -1), jnp.where(place == slots, sizes, 0)], axis=-1
-    ).reshape(groups * SLOT, 2)
-
-    def used(near, degree):
-        column = lax.broadcasted_iota(jnp.int32, near.shape, 1)
-        return jnp.where(column < degree[:, None], near, -1)
-
-    def moved(index):
-        return index // slots * SLOT + lax.rem(index, slots)
-
-    ids_one = jnp.concatenate([used(moved(near_one), degree_one), moved(self_ids)[:, None]], axis=1)
     vmem = pl.BlockSpec(memory_space=pltpu.VMEM)
     hbm = pl.BlockSpec(memory_space=pl.ANY)
     lanes = min(128, width)
     c1, c2, c3 = 4, 2, 2
     dma = pltpu.SemaphoreType.DMA
     chips = groups // 2
-    scratch = [
+    scratch = [pltpu.VMEM((rows, SLOT), jnp.int32) for rows in (outer, mid, seeds)]
+    scratch += [
+        pltpu.VMEM((groups * SLOT, lanes), F32),
         pltpu.VMEM(features.shape, BF16),
         pltpu.VMEM((groups * SLOT, features.shape[0]), BF16),
         pltpu.VMEM((stores, groups * SLOT, width), BF16),
@@ -408,24 +430,27 @@
     scratch += [dma((1 + 6 * stores,)), dma((stores,)), dma((stores,))]
     scratch += [dma((3, chunks)) for chunks in (c1, c1, c2, c2, c3, c3)]
     scratch += [dma((2, 3)), dma((2, 3)), dma((3,)), dma((3,)), dma((3,)), dma((3,))]
-    return pl.pallas_call(
+    shapes = (
+        jax.ShapeDtypeStruct((seeds, width), BF16),
+        jax.ShapeDtypeStruct((height, width), F32),
+        jax.ShapeDtypeStruct((height, width), F32),
+        jax.ShapeDtypeStruct((height, width), F32),
+    )
+    results = pl.pallas_call(
         functools.partial(kernel, stores, groups, slots),
-        out_shape=(
-            jax.ShapeDtypeStruct((seeds, width), BF16),
-            jax.ShapeDtypeStruct((height, width), F32),
-            jax.ShapeDtypeStruct((height, width), F32),
-            jax.ShapeDtypeStruct((height, width), F32),
-        ),
-        in_specs=[vmem] * 5 + [hbm] * 4,
+        out_shape=shapes,
+        in_specs=[vmem] * 10 + [hbm] * 4,
         out_specs=(vmem,) * 4,
         scratch_shapes=scratch,
         compiler_params=pltpu.CompilerParams(
             collective_id=0, has_side_effects=True, vmem_limit_bytes=60 * 1024 * 1024
         ),
     )(
-        ids, ids_one, used(near_two, degree_two), used(near_three, degree_three), cotangent,
-        features, weight_one, weight_two, weight_three,
+        jnp.transpose(sent_ids, (2, 0, 1)), block_sizes, self_ids,
+        near_one.T, degree_one, near_two.T, degree_two, near_three.T, degree_three,
+        cotangent, features, weight_one, weight_two, weight_three,
     )
+    return pl.pallas_call(copies, out_shape=shapes, in_specs=[vmem] * 4, out_specs=(vmem,) * 4)(*results)
 
 
 def solution(mesh):

time: 143 us -> 127 us (0.89)
  local copies, waits for them, and re-layouts: 11.2 us -> 0 us
  other arithmetic: 5.14 us -> 0 us
    unnamed x7 -> x0, local copies, waits for them, and re-layouts: 8.34 us -> none
    select_n x5 -> x0, other arithmetic: 4.41 us -> none  [the longest x3 3.74 us: used(): return jnp.where(column < degree[:, None], near, -1)]
    pallas_call x0 -> x1, Pallas kernels: none -> 1.66 us  [run(): pl.pallas_call(copies, out_shape=shapes, in_specs=[vmem] * 4, out_specs=(...]
where the time goes in v2:
time: 127 us; the launch traced here: 126 us
  Pallas kernels  125 us (98%)
    pallas_call x1, Pallas kernels, run(): pl.pallas_call(functools.partial(kernel, stores, groups, slots), out_shap...  123 us

profile of v2, /device:TPU:3, one launch (start us, length us, event | category | flops | bytes accessed | tf_op | source)
XLA Modules:
  0.0 125.7 jit_solution(12676554473599908153)
XLA Ops:
  0.6 123.4 %shard_map.165 = (bf16[192,256]{1,0:T(8,128)(2,1)}, f32[64,256]{1,0:T(8,128)}, f32[64,256]{1,0:T(8,128)}, f32[64,256]{1,0:T(8,128)}) custom-call(s32[12,1,32]{2,1,0:T(1,128)} %bitcast.7, s32[1,32]{1,0:T(1,128)} %sizes.1, s32[768]{0:T(1024)} %self_ids.1, s32[10,768]{1,0:T(8,128)} %bitcast.4, s32[768]{0:T(1024)} %degree_one.1, s32[10,384]{1,0:T(8,128)} %bitcast.5, ...), custom_call_target="tpu_custom_call" | custom-call | tf_op jit(solution)/shard_map/pallas_call | solution.py:439
  124.0 1.7 %shard_map.166 = (bf16[192,256]{1,0:T(8,128)(2,1)}, f32[64,256]{1,0:T(8,128)}, f32[64,256]{1,0:T(8,128)}, f32[64,256]{1,0:T(8,128)}) custom-call(bf16[192,256]{1,0:T(8,128)(2,1)} %get-tuple-element.8.refs_0_, f32[64,256]{1,0:T(8,128)} %get-tuple-element.9.refs_1_, f32[64,256]{1,0:T(8,128)} %get-tuple-element.10.refs_2_, f32[64,256]{1,0:T(8,128)} %get-tuple-element.11.refs_3_), custom_call_target="tpu_custom_call" | custom-call | tf_op jit(solution)/shard_map/pallas_call | solution.py:453

commit v3 on v2

--- a/solution.py
+++ b/solution.py
@@ -55,13 +55,14 @@
     sent, sizes, self_ids, near_one_t, degree_one, near_two_t, degree_two, near_three_t, degree_three,
     cot, feat_hbm, one_hbm, two_hbm, three_hbm,
     emb_out, one_out, two_out, three_out,
-    near_one, near_two, near_three, extra, feat, hot, picked, arrived, filled, tile_one, tile_self, tile_two, tile_three,
-    w_one, w_two, w_three, j_one, j_two, j_three, pre_one, pre_two, hid_one, hid_two,
-    sp3_send, sp3_recv, sp2_send, sp2_recv, below3, dpre_two, dpre_one, full,
-    px_send, px_recv, blk, rr,
-    load_sem, in_send, in_recv,
-    ag1_send, ag1_recv, ag2_send, ag2_recv, ag3_send, ag3_recv,
-    sp_send_sem, sp_recv_sem, px_ssem, px_rsem, rr_ssem, rr_rsem,
+    near_one, near_two, near_three, extra, feat, hot, picked, arrived, filled,
+    tile_one, tile_self, tile_two, tile_three, w_one, w_rows,
+    j_one, j_two, j_three, pre_one, pre_two, hid_one, hid_two, cots, dpres, spread_two, below3, dpre_one,
+    part_two, got_two, part_three, got_three,
+    full, px_send, px_recv, blk, rr, move_send, move_recv,
+    load_sem, in_send, in_recv, ag1_send, ag1_recv, agd_send, agd_recv,
+    cot_ssem, cot_rsem, wz_ssem, wz_rsem, wp_ssem, wp_rsem, ws_ssem, ws_rsem,
+    rs_ssem, rs_rsem, px_ssem, px_rsem, rr_ssem, rr_rsem, mv_ssem, mv_rsem,
 ):
     devices = stores * groups
     z = lax.axis_index("store")
@@ -69,10 +70,13 @@
     me = z * groups + t
     chip, core = t // 2, lax.rem(t, 2)
     chips = groups // 2
+    sibling = t + 1 - 2 * core
     right, left, across = (lax.rem(z + k, stores) for k in (1, 3, 2))
+    others = ((across, 2), (right, 0), (left, 1))
     width = cot.shape[1]
     seeds, mid, outer = cot.shape[0], near_two.shape[0], near_one.shape[0]
     cells = devices * SLOT
+    fan = near_two_t.shape[0]
     pending = []
 
     def remote(src, dst, send_sem, recv_sem, store, trainer):
@@ -95,18 +99,24 @@
 
     lax.fori_loop(1, devices, greet, 0)
 
+    share = w_rows.shape[4]
+
+    def piece_of(hbm, store):
+        return hbm.at[pl.ds(pl.multiple_of(core * stores * width + store * width + chip * share, share), share), :]
+
     loads = [pltpu.make_async_copy(feat_hbm, feat, load_sem.at[0])]
-    for place, (hbm, held) in enumerate(((one_hbm, w_one), (two_hbm, w_two), (three_hbm, w_three))):
-        for store in range(stores):
-            for half in range(2):
-                source = half * stores * width + store * width
-                loads.append(
-                    pltpu.make_async_copy(
-                        hbm.at[pl.ds(source, width), :],
-                        held.at[store, pl.ds(half * width, width), :],
-                        load_sem.at[1 + (place * stores + store) * 2 + half],
-                    )
+    for place, hbm in enumerate((two_hbm, three_hbm)):
+        loads.append(pltpu.make_async_copy(piece_of(hbm, z), w_rows.at[place, core, chip, z], load_sem.at[1 + place]))
+    loads.append(pltpu.make_async_copy(cot, cots.at[z], load_sem.at[3]))
+    for store in range(stores):
+        for half in range(2):
+            loads.append(
+                pltpu.make_async_copy(
+                    one_hbm.at[pl.ds((half * stores + store) * width, width), :],
+                    w_one.at[store, pl.ds(half * width, width), :],
+                    load_sem.at[4 + store * 2 + half],
                 )
+            )
     for load in loads:
         load.start()
 
@@ -125,6 +135,14 @@
     loads[0].wait()
     pl.semaphore_wait(barrier, devices - 1)
 
+    for store, place in others:
+        remote(cot, cots.at[z], cot_ssem.at[place], cot_rsem.at[place], store, t).start()
+        pending.append(lambda place=place: await_bytes(cot, cot_ssem.at[place]))
+        for number, hbm in enumerate((two_hbm, three_hbm)):
+            spot = w_rows.at[number, core, chip, z]
+            remote(piece_of(hbm, store), spot, wz_ssem.at[number, place], wz_rsem.at[number, place], store, t).start()
+            pending.append(lambda number=number, place=place, spot=spot: await_bytes(spot, wz_ssem.at[number, place]))
+
     def fetch(index, carry):
         store = lax.rem(z + index, stores)
         columns = pl.ds(pl.multiple_of(store * width, width), width)
@@ -165,28 +183,6 @@
     for load in loads[1:]:
         load.wait()
 
-    others = ((right, 0), (left, 1), (across, 2))
-
-    def send_spread(dpre, weight, send, recv, number):
-        for store, place in others:
-            send[place] = dot(dpre[...], weight[store], 1, 1).astype(BF16)
-            remote(
-                send.at[place], recv.at[place],
-                sp_send_sem.at[number, place], sp_recv_sem.at[number, place], store, t,
-            ).start()
-            pending.append(lambda place=place: await_bytes(send.at[place], sp_send_sem.at[number, place]))
-
-    def take_spread(dpre, weight, recv, number):
-        total = dot(dpre[...], weight[z], 1, 1)
-        for place in range(3):
-            await_bytes(recv.at[place], sp_recv_sem.at[number, place])
-            total = total + recv[place].astype(F32)
-        return total
-
-    send_spread(cot, w_three, sp3_send, sp3_recv, 0)
-
-    fan = near_two_t.shape[0]
-
     def moved(index):
         return index + (SLOT - slots) * ((index * ((1 << 19) // slots + 1)) >> 19)
 
@@ -208,21 +204,19 @@
     def counted(near):
         return 1.0 + jnp.sum(jnp.where(near[...] >= 0, 1.0, 0.0), axis=1, keepdims=True)
 
-    def spread_below(total, near, tile, below_rows):
+    def spread_below(total, near, tile):
         rows = near.shape[0]
         scaled = (total[:, width:] / counted(near)).astype(BF16)
         below = dot(tile[...], scaled, 0, 0)
         upper = below[:rows] + (total[:, :width] + scaled.astype(F32))
         return jnp.concatenate([upper, below[rows:]], axis=0)
 
-    below3[...] = spread_below(take_spread(cot, w_three, sp3_recv, 0), near_three, tile_three, mid)
-
     def start_gather(held, index, rows, send_sem, recv_sem):
         piece = held.at[z, rows_at(index, rows), :]
         remote(piece, piece, send_sem.at[0, index], recv_sem.at[0, index], right, t).start()
         remote(piece, piece, send_sem.at[1, index], recv_sem.at[1, index], left, t).start()
 
-    def take_gather(held, chunks, rows, send_sem, recv_sem, use):
+    def take_gather(held, chunks, rows, send_sem, recv_sem, use, between):
         for index in range(chunks):
             here = rows_at(index, rows)
             for side, (source, onward) in enumerate(((left, right), (right, left))):
@@ -232,6 +226,7 @@
                     remote(piece, piece, send_sem.at[2, index], recv_sem.at[2, index], onward, t).start()
             for source in (left, right):
                 use(source, here)
+        between()
         for index in range(chunks):
             here = rows_at(index, rows)
             await_bytes(held.at[across, here, :], recv_sem.at[2, index])
@@ -244,9 +239,6 @@
                     )
                 )
 
-    for store in range(stores):
-        await_bytes(arrived.at[pl.ds(store * groups * SLOT, groups * SLOT), :], in_recv.at[store])
-
     def mark(index, carry):
         here = rows_at(index, SLOT)
         block = arrived[here, 0 : filled.shape[1]].astype(F32)
@@ -254,7 +246,9 @@
         filled[here, :] = jnp.where(place < block[slots : slots + 1, :], 1.0, 0.0).astype(BF16)
         return carry
 
-    lax.fori_loop(0, devices, mark, 0)
+    for store in range(stores):
+        await_bytes(arrived.at[pl.ds(store * groups * SLOT, groups * SLOT), :], in_recv.at[store])
+        lax.fori_loop(store * groups, (store + 1) * groups, mark, 0)
 
     chunks_one = ag1_send.shape[1]
     rows_one = outer // chunks_one
@@ -272,62 +266,117 @@
 
     lax.fori_loop(0, chunks_one, layer_one, 0)
 
+    for number in range(2):
+        for store, place in others:
+            await_bytes(w_rows.at[number, core, chip, store], wz_rsem.at[number, place])
+
+        def pass_on(index, carry, number=number):
+            target = lax.rem(chip + index, chips)
+            spot = w_rows.at[number, core, chip]
+            remote(spot, spot, wp_ssem.at[number], wp_rsem.at[number], z, target * 2 + core).start()
+            return carry
+
+        lax.fori_loop(1, chips, pass_on, 0)
+        pending.append(lambda number=number: await_bytes(w_rows.at[number, core, pl.ds(0, chips - 1)], wp_ssem.at[number]))
+
     def use_one(source, here):
         pre_one[here, :] += dot(j_one[source, here, :], w_one[source])
 
-    take_gather(j_one, chunks_one, rows_one, ag1_send, ag1_recv, use_one)
+    def swap_weights():
+        for number in range(2):
+            spot = w_rows.at[number, core]
+            await_bytes(w_rows.at[number, core, pl.ds(0, chips - 1)], wp_rsem.at[number])
+            remote(spot, spot, ws_ssem.at[number], ws_rsem.at[number], z, sibling).start()
+            pending.append(lambda spot=spot, number=number: await_bytes(spot, ws_ssem.at[number]))
+
+    take_gather(j_one, chunks_one, rows_one, ag1_send, ag1_recv, use_one, swap_weights)
     hid_one[...] = (pre_one[...] * jax.nn.sigmoid(pre_one[...])).astype(BF16)
-
-    def join(hidden, near, tile, joined, chunks, send_sem, recv_sem):
+    for number in range(2):
+        await_bytes(w_rows.at[number, 1 - core], ws_rsem.at[number])
+
+    def rows_of(number, store):
+        return w_rows[number, :, :, store].reshape(2 * width, width)
+
+    def join(hidden, near, tile, joined):
         rows = near.shape[0]
         own = hidden[0:rows, :]
         mean = (own.astype(F32) + dot(tile[...], hidden[...])) / counted(near)
-        joined[z] = jnp.concatenate([own, mean.astype(BF16)], axis=1)
-        for index in range(chunks):
-            start_gather(joined, index, rows // chunks, send_sem, recv_sem)
-
-    chunks_two, chunks_three = ag2_send.shape[1], ag3_send.shape[1]
-    rows_two, rows_three = mid // chunks_two, seeds // chunks_three
-    join(hid_one, near_two, tile_two, j_two, chunks_two, ag2_send, ag2_recv)
-    pre_two[...] = dot(j_two[z], w_two[z])
-
-    def use_two(source, here):
-        pre_two[here, :] += dot(j_two[source, here, :], w_two[source])
-
-    take_gather(j_two, chunks_two, rows_two, ag2_send, ag2_recv, use_two)
-    dpre_two[...] = (below3[...] * slope(pre_two[...])).astype(BF16)
-    send_spread(dpre_two, w_two, sp2_send, sp2_recv, 1)
+        joined[...] = jnp.concatenate([own, mean.astype(BF16)], axis=1)
+
+    def send_partials(joined, number, part, got):
+        for store, place in others:
+            part[place] = dot(joined[...], rows_of(number, store)).astype(BF16)
+            remote(
+                part.at[place], got.at[place], rs_ssem.at[number, place], rs_rsem.at[number, place], store, t
+            ).start()
+            pending.append(lambda place=place: await_bytes(part.at[place], rs_ssem.at[number, place]))
+
+    def take_partials(joined, number, got):
+        total = dot(joined[...], rows_of(number, z))
+        for place in range(3):
+            await_bytes(got.at[place], rs_rsem.at[number, place])
+            total = total + got[place].astype(F32)
+        return total
+
+    join(hid_one, near_two, tile_two, j_two)
+    send_partials(j_two, 0, part_two, got_two)
+    for store, place in others:
+        await_bytes(cots.at[store], cot_rsem.at[place])
+    spread = dot(cots[0], rows_of(1, 0), 1, 1)
+    for store in range(1, stores):
+        spread = spread + dot(cots[store], rows_of(1, store), 1, 1)
+    below3[...] = spread_below(spread, near_three, tile_three)
+    pre_two[...] = take_partials(j_two, 0, got_two)
+    dpres[z] = (below3[...] * slope(pre_two[...])).astype(BF16)
+    chunks_two = agd_send.shape[1]
+    rows_two = mid // chunks_two
+    for index in range(chunks_two):
+        start_gather(dpres, index, rows_two, agd_send, agd_recv)
     hid_two[...] = (pre_two[...] * jax.nn.sigmoid(pre_two[...])).astype(BF16)
-    join(hid_two, near_three, tile_three, j_three, chunks_three, ag3_send, ag3_recv)
-
-    height = full.shape[1]
+    join(hid_two, near_three, tile_three, j_three)
+
+    height = full.shape[2]
     per_slice = width // height
 
-    def start_grad(number, joined, dpre):
+    def pack(number):
+        def body(index, carry):
+            px_send[number, index] = full[number, index * 2 + 1 - core].astype(BF16)
+            return carry
+
+        lax.fori_loop(0, chips, body, 0)
+        remote(
+            px_send.at[number], px_recv.at[number], px_ssem.at[number], px_rsem.at[number], z, sibling
+        ).start()
+        pending.append(lambda: await_bytes(px_send.at[number], px_ssem.at[number]))
+
+    def grad_of_columns(number, joined, dpre):
         def products(store, carry):
             part = dot(joined[store], dpre[...], 0, 0)
             for half in range(2):
                 for index in range(per_slice):
                     start = half * width + index * height
-                    full[half * (groups // 2) + store * per_slice + index] = part[start : start + height, :]
+                    full[number, half * (groups // 2) + store * per_slice + index] = part[start : start + height, :]
             return carry
 
         lax.fori_loop(0, stores, products, 0)
-
-        def pack(index, carry):
-            px_send[number, index] = full[index * 2 + 1 - core].astype(BF16)
+        pack(number)
+
+    def grad_of_rows(number, joined, columns):
+        def products(store, carry):
+            part = dot(joined[...], columns[store], 0, 0)
+            for index in range(2 * per_slice):
+                full[number, index * stores + store] = part[index * height : (index + 1) * height, :]
             return carry
 
-        lax.fori_loop(0, chips, pack, 0)
-        remote(
-            px_send.at[number], px_recv.at[number], px_ssem.at[number], px_rsem.at[number], z, t + 1 - 2 * core
-        ).start()
-        pending.append(lambda: await_bytes(px_send.at[number], px_ssem.at[number]))
+        lax.fori_loop(0, stores, products, 0)
+        pack(number)
+
+    def share_grad(number):
         await_bytes(px_recv.at[number], px_rsem.at[number])
 
-        def spread(index, carry):
+        def body(index, carry):
             target = lax.rem(chip + index, chips)
-            total = full[target * 2 + core] + px_recv[number, target].astype(F32)
+            total = full[number, target * 2 + core] + px_recv[number, target].astype(F32)
             blk[number, target] = total.astype(BF16)
 
             @pl.when(index > 0)
@@ -343,35 +392,62 @@
 
             return carry
 
-        lax.fori_loop(0, chips, spread, 0)
+        lax.fori_loop(0, chips, body, 0)
         pending.append(lambda: await_bytes(blk.at[number, pl.ds(0, chips - 1)], rr_ssem.at[number]))
 
-    def finish_grad(number, out):
+    def summed(number):
         await_bytes(rr.at[number, pl.ds(0, chips - 1)], rr_rsem.at[number])
-        out[...] = jnp.sum(rr[number].astype(F32), axis=0)
-
-    start_grad(1, j_two, dpre_two)
-    below2 = spread_below(take_spread(dpre_two, w_two, sp2_recv, 1), near_two, tile_two, outer)
+        return jnp.sum(rr[number].astype(F32), axis=0)
+
+    block, to_store = t // stores, lax.rem(t, stores)
+    to_trainer = jnp.where(
+        block < per_slice, z * per_slice + block, groups // 2 + z * per_slice + block - per_slice
+    )
+    moves = jnp.logical_or(to_store != z, to_trainer != t)
+
+    def move(number):
+        move_send[number] = summed(number)
+        sems = mv_ssem.at[number], mv_rsem.at[number]
+
+        @pl.when(moves)
+        def _():
+            remote(move_send.at[number], move_recv.at[number], *sems, to_store, to_trainer).start()
+
+        @pl.when(jnp.logical_not(moves))
+        def _():
+            pltpu.make_async_copy(move_send.at[number], move_recv.at[number], mv_rsem.at[number]).start()
+
+        def leave():
+            @pl.when(moves)
+            def _():
+                await_bytes(move_send.at[number], mv_ssem.at[number])
+
+        pending.append(leave)
+
+    def take_move(number, out):
+        await_bytes(move_recv.at[number], mv_rsem.at[number])
+        out[...] = move_recv[number]
+
+    grad_of_rows(1, j_three, cots)
+    spread_two[...] = dot(dpres[z], rows_of(0, z), 1, 1)
+
+    def use_two(source, here):
+        spread_two[here, :] += dot(dpres[source, here, :], rows_of(0, source), 1, 1)
+
+    take_gather(dpres, chunks_two, rows_two, agd_send, agd_recv, use_two, lambda: share_grad(1))
+    grad_of_rows(0, j_two, dpres)
+    below2 = spread_below(spread_two[...], near_two, tile_two)
     dpre_one[...] = (below2 * slope(pre_one[...])).astype(BF16)
-    start_grad(0, j_one, dpre_one)
-
-    emb = [dot(j_three[z], w_three[z])]
-
-    def use_three(source, here):
-        emb[0] = emb[0] + dot(j_three[source], w_three[source])
-
-    def keep(source, here):
-        return None
-
-    take_gather(j_three, chunks_three, rows_three, ag3_send, ag3_recv, keep)
-    for source in (left, right, across):
-        use_three(source, None)
-    emb_out[...] = emb[0].astype(BF16)
-    start_grad(2, j_three, cot)
-
-    finish_grad(1, two_out)
-    finish_grad(0, one_out)
-    finish_grad(2, three_out)
+    share_grad(0)
+    grad_of_columns(2, j_one, dpre_one)
+    send_partials(j_three, 1, part_three, got_three)
+    move(1)
+    share_grad(2)
+    emb_out[...] = take_partials(j_three, 1, got_three).astype(BF16)
+    move(0)
+    take_move(1, three_out)
+    one_out[...] = summed(2)
+    take_move(0, two_out)
 
     for leave in pending:
         leave()
@@ -399,7 +475,7 @@
     vmem = pl.BlockSpec(memory_space=pltpu.VMEM)
     hbm = pl.BlockSpec(memory_space=pl.ANY)
     lanes = min(128, width)
-    c1, c2, c3 = 4, 2, 2
+    chunks_one, chunks_two = 4, 2
     dma = pltpu.SemaphoreType.DMA
     chips = groups // 2
     scratch = [pltpu.VMEM((rows, SLOT), jnp.int32) for rows in (outer, mid, seeds)]
@@ -414,22 +490,29 @@
         pltpu.VMEM((outer, cells), BF16),
         pltpu.VMEM((mid, outer), BF16),
         pltpu.VMEM((seeds, mid), BF16),
+        pltpu.VMEM((stores, 2 * width, width), BF16),
+        pltpu.VMEM((2, 2, chips, stores, width // chips, width), BF16),
+        pltpu.VMEM((stores, outer, 2 * width), BF16),
+        pltpu.VMEM((mid, 2 * width), BF16),
+        pltpu.VMEM((seeds, 2 * width), BF16),
+        pltpu.VMEM((outer, width), F32),
+        pltpu.VMEM((mid, width), F32),
+        pltpu.VMEM((outer, width), BF16),
+        pltpu.VMEM((mid, width), BF16),
+        pltpu.VMEM((stores, seeds, width), BF16),
+        pltpu.VMEM((stores, mid, width), BF16),
+        pltpu.VMEM((mid, 2 * width), F32),
+        pltpu.VMEM((mid, width), F32),
+        pltpu.VMEM((outer, width), BF16),
     ]
-    scratch += [pltpu.VMEM((stores, 2 * width, width), BF16)] * 3
-    scratch += [pltpu.VMEM((stores, rows, 2 * width), BF16) for rows in (outer, mid, seeds)]
-    scratch += [pltpu.VMEM((rows, width), F32) for rows in (outer, mid)]
-    scratch += [pltpu.VMEM((rows, width), BF16) for rows in (outer, mid)]
-    scratch += [pltpu.VMEM((3, seeds, 2 * width), BF16)] * 2 + [pltpu.VMEM((3, mid, 2 * width), BF16)] * 2
-    scratch += [
-        pltpu.VMEM((mid, width), F32),
-        pltpu.VMEM((mid, width), BF16),
-        pltpu.VMEM((outer, width), BF16),
-        pltpu.VMEM((groups, height, width), F32),
-    ]
+    scratch += [pltpu.VMEM((3, mid, width), BF16)] * 2 + [pltpu.VMEM((3, seeds, width), BF16)] * 2
+    scratch += [pltpu.VMEM((3, groups, height, width), F32)]
     scratch += [pltpu.VMEM((3, chips, height, width), BF16)] * 4
-    scratch += [dma((1 + 6 * stores,)), dma((stores,)), dma((stores,))]
-    scratch += [dma((3, chunks)) for chunks in (c1, c1, c2, c2, c3, c3)]
-    scratch += [dma((2, 3)), dma((2, 3)), dma((3,)), dma((3,)), dma((3,)), dma((3,))]
+    scratch += [pltpu.VMEM((2, height, width), F32)] * 2
+    scratch += [dma((4 + 2 * stores,)), dma((stores,)), dma((stores,))]
+    scratch += [dma((3, chunks)) for chunks in (chunks_one, chunks_one, chunks_two, chunks_two)]
+    scratch += [dma((3,))] * 2 + [dma((2, 3))] * 2 + [dma((2,))] * 4 + [dma((2, 3))] * 2
+    scratch += [dma((3,))] * 4 + [dma((2,))] * 2
     shapes = (
         jax.ShapeDtypeStruct((seeds, width), BF16),
         jax.ShapeDtypeStruct((height, width), F32),

time: 127 us -> 115 us (0.906)
  the two profiles are of different devices: /device:TPU:3 before, /device:TPU:14 now
where the time goes in v3:
time: 115 us
  Pallas kernels  114 us (99%)
    pallas_call x1, Pallas kernels, run(): pl.pallas_call(functools.partial(kernel, stores, groups, slots), out_shap...  112 us

profile of v3, /device:TPU:14, one launch (start us, length us, event | category | flops | bytes accessed | tf_op | source)
XLA Modules:
  0.0 114.7 jit_solution(1499349842755297684)
XLA Ops:
  0.6 112.4 %shard_map.165 = (bf16[192,256]{1,0:T(8,128)(2,1)}, f32[64,256]{1,0:T(8,128)}, f32[64,256]{1,0:T(8,128)}, f32[64,256]{1,0:T(8,128)}) custom-call(s32[12,1,32]{2,1,0:T(1,128)} %bitcast.7, s32[1,32]{1,0:T(1,128)} %sizes.1, s32[768]{0:T(1024)} %self_ids.1, s32[10,768]{1,0:T(8,128)} %bitcast.4, s32[768]{0:T(1024)} %degree_one.1, s32[10,384]{1,0:T(8,128)} %bitcast.5, ...), custom_call_target="tpu_custom_call" | custom-call | tf_op jit(solution)/shard_map/pallas_call | solution.py:522
  113.0 1.7 %shard_map.166 = (bf16[192,256]{1,0:T(8,128)(2,1)}, f32[64,256]{1,0:T(8,128)}, f32[64,256]{1,0:T(8,128)}, f32[64,256]{1,0:T(8,128)}) custom-call(bf16[192,256]{1,0:T(8,128)(2,1)} %get-tuple-element.8.refs_0_, f32[64,256]{1,0:T(8,128)} %get-tuple-element.9.refs_1_, f32[64,256]{1,0:T(8,128)} %get-tuple-element.10.refs_2_, f32[64,256]{1,0:T(8,128)} %get-tuple-element.11.refs_3_), custom_call_target="tpu_custom_call" | custom-call | tf_op jit(solution)/shard_map/pallas_call | solution.py:536

commit v4 on v3

--- a/solution.py
+++ b/solution.py
@@ -1,4 +1,5 @@
 import functools
+import math
 
 import jax
 import jax.numpy as jnp
@@ -59,10 +60,10 @@
     tile_one, tile_self, tile_two, tile_three, w_one, w_rows,
     j_one, j_two, j_three, pre_one, pre_two, hid_one, hid_two, cots, dpres, spread_two, below3, dpre_one,
     part_two, got_two, part_three, got_three,
-    full, px_send, px_recv, blk, rr, move_send, move_recv,
+    full, px_send, px_recv, blk, rr, line, thin, last, move_send, move_recv,
     load_sem, in_send, in_recv, ag1_send, ag1_recv, agd_send, agd_recv,
     cot_ssem, cot_rsem, wz_ssem, wz_rsem, wp_ssem, wp_rsem, ws_ssem, ws_rsem,
-    rs_ssem, rs_rsem, px_ssem, px_rsem, rr_ssem, rr_rsem, mv_ssem, mv_rsem,
+    rs_ssem, rs_rsem, px_ssem, px_rsem, rr_ssem, rr_rsem, ls_ssem, ls_rsem, mv_ssem, mv_rsem,
 ):
     devices = stores * groups
     z = lax.axis_index("store")
@@ -303,34 +304,38 @@
         mean = (own.astype(F32) + dot(tile[...], hidden[...])) / counted(near)
         joined[...] = jnp.concatenate([own, mean.astype(BF16)], axis=1)
 
-    def send_partials(joined, number, part, got):
-        for store, place in others:
-            part[place] = dot(joined[...], rows_of(number, store)).astype(BF16)
-            remote(
-                part.at[place], got.at[place], rs_ssem.at[number, place], rs_rsem.at[number, place], store, t
-            ).start()
-            pending.append(lambda place=place: await_bytes(part.at[place], rs_ssem.at[number, place]))
-
-    def take_partials(joined, number, got):
-        total = dot(joined[...], rows_of(number, z))
+    def send_partials(joined, number, part, got, chunks):
+        rows = part.shape[1] // chunks
+        for index in range(chunks):
+            here = pl.ds(index * rows, rows)
+            for store, place in others:
+                part[place, here, :] = dot(joined[here, :], rows_of(number, store)).astype(BF16)
+                sems = rs_ssem.at[number, index, place], rs_rsem.at[number, index, place]
+                remote(part.at[place, here, :], got.at[place, here, :], *sems, store, t).start()
+                pending.append(lambda place=place, here=here, sem=sems[0]: await_bytes(part.at[place, here, :], sem))
+
+    def take_partials(joined, number, got, index, rows):
+        here = pl.ds(index * rows, rows)
+        total = dot(joined[here, :], rows_of(number, z))
         for place in range(3):
-            await_bytes(got.at[place], rs_rsem.at[number, place])
-            total = total + got[place].astype(F32)
+            await_bytes(got.at[place, here, :], rs_rsem.at[number, index, place])
+            total = total + got[place, here, :].astype(F32)
         return total
 
     join(hid_one, near_two, tile_two, j_two)
-    send_partials(j_two, 0, part_two, got_two)
+    chunks_two = agd_send.shape[1]
+    rows_two = mid // chunks_two
+    send_partials(j_two, 0, part_two, got_two, chunks_two)
     for store, place in others:
         await_bytes(cots.at[store], cot_rsem.at[place])
     spread = dot(cots[0], rows_of(1, 0), 1, 1)
     for store in range(1, stores):
         spread = spread + dot(cots[store], rows_of(1, store), 1, 1)
     below3[...] = spread_below(spread, near_three, tile_three)
-    pre_two[...] = take_partials(j_two, 0, got_two)
-    dpres[z] = (below3[...] * slope(pre_two[...])).astype(BF16)
-    chunks_two = agd_send.shape[1]
-    rows_two = mid // chunks_two
     for index in range(chunks_two):
+        here = rows_at(index, rows_two)
+        pre_two[here, :] = take_partials(j_two, 0, got_two, index, rows_two)
+        dpres[z, here, :] = (below3[here, :] * slope(pre_two[here, :])).astype(BF16)
         start_gather(dpres, index, rows_two, agd_send, agd_recv)
     hid_two[...] = (pre_two[...] * jax.nn.sigmoid(pre_two[...])).astype(BF16)
     join(hid_two, near_three, tile_three, j_three)
@@ -371,33 +376,68 @@
         lax.fori_loop(0, stores, products, 0)
         pack(number)
 
-    def share_grad(number):
+    side = rr.shape[2]
+    place_x, place_y = chip // side, lax.rem(chip, side)
+    spots = (place_x, place_y)
+
+    def partner(way, index):
+        target = lax.rem(spots[way] + index, side)
+        column = (target, place_y) if way == 0 else (place_x, target)
+        return target, (column[0] * side + column[1]) * 2 + core
+
+    def share_first(number):
         await_bytes(px_recv.at[number], px_rsem.at[number])
 
         def body(index, carry):
-            target = lax.rem(chip + index, chips)
-            total = full[number, target * 2 + core] + px_recv[number, target].astype(F32)
-            blk[number, target] = total.astype(BF16)
-
-            @pl.when(index > 0)
-            def _():
+            total = full[number, index * 2 + core] + px_recv[number, index].astype(F32)
+            first, second = index // side, lax.rem(index, side)
+            blk[number, 0, first, second] = total[: height // 2].astype(BF16)
+            blk[number, 1, second, first] = total[height // 2 :].astype(BF16)
+            return carry
+
+        lax.fori_loop(0, chips, body, 0)
+        for way in range(2):
+            for index in range(1, side):
+                target, trainer = partner(way, index)
                 remote(
-                    blk.at[number, target], rr.at[number, chip],
-                    rr_ssem.at[number], rr_rsem.at[number], z, target * 2 + core,
+                    blk.at[number, way, target], rr.at[number, way, index],
+                    rr_ssem.at[number, way, index], rr_rsem.at[number, way, index], z, trainer,
                 ).start()
-
-            @pl.when(index == 0)
-            def _():
-                rr[number, chip] = total.astype(BF16)
-
-            return carry
-
-        lax.fori_loop(0, chips, body, 0)
-        pending.append(lambda: await_bytes(blk.at[number, pl.ds(0, chips - 1)], rr_ssem.at[number]))
+                pending.append(
+                    lambda way=way, index=index, target=target: await_bytes(
+                        blk.at[number, way, target], rr_ssem.at[number, way, index]
+                    )
+                )
+
+    def share_second(number):
+        for way in range(2):
+            total = blk[number, way, spots[way]].astype(F32)
+            for index in range(1, side):
+                await_bytes(rr.at[number, way, index], rr_rsem.at[number, way, index])
+                total = total + rr[number, way, index].astype(F32)
+            line[number, way] = total
+            thin[number, way] = total.astype(BF16)
+            for index in range(1, side):
+                target, trainer = partner(1 - way, index)
+                remote(
+                    thin.at[number, way, target], last.at[number, way, index],
+                    ls_ssem.at[number, way, index], ls_rsem.at[number, way, index], z, trainer,
+                ).start()
+                pending.append(
+                    lambda way=way, index=index, target=target: await_bytes(
+                        thin.at[number, way, target], ls_ssem.at[number, way, index]
+                    )
+                )
 
     def summed(number):
-        await_bytes(rr.at[number, pl.ds(0, chips - 1)], rr_rsem.at[number])
-        return jnp.sum(rr[number].astype(F32), axis=0)
+        halves = []
+        for way in range(2):
+            total = line[number, way, spots[1 - way]]
+            for index in range(1, side):
+                await_bytes(last.at[number, way, index], ls_rsem.at[number, way, index])
+                total = total + last[number, way, index].astype(F32)
+            halves.append(total)
+        return jnp.concatenate(halves, axis=0)
 
     block, to_store = t // stores, lax.rem(t, stores)
     to_trainer = jnp.where(
@@ -406,7 +446,7 @@
     moves = jnp.logical_or(to_store != z, to_trainer != t)
 
     def move(number):
-        move_send[number] = summed(number)
+        move_send[number] = summed(number).astype(BF16)
         sems = mv_ssem.at[number], mv_rsem.at[number]
 
         @pl.when(moves)
@@ -426,7 +466,7 @@
 
     def take_move(number, out):
         await_bytes(move_recv.at[number], mv_rsem.at[number])
-        out[...] = move_recv[number]
+        out[...] = move_recv[number].astype(F32)
 
     grad_of_rows(1, j_three, cots)
     spread_two[...] = dot(dpres[z], rows_of(0, z), 1, 1)
@@ -434,20 +474,23 @@
     def use_two(source, here):
         spread_two[here, :] += dot(dpres[source, here, :], rows_of(0, source), 1, 1)
 
-    take_gather(dpres, chunks_two, rows_two, agd_send, agd_recv, use_two, lambda: share_grad(1))
+    take_gather(dpres, chunks_two, rows_two, agd_send, agd_recv, use_two, lambda: share_first(1))
+    send_partials(j_three, 1, part_three, got_three, 1)
     grad_of_rows(0, j_two, dpres)
     below2 = spread_below(spread_two[...], near_two, tile_two)
     dpre_one[...] = (below2 * slope(pre_one[...])).astype(BF16)
-    share_grad(0)
+    share_first(0)
     grad_of_columns(2, j_one, dpre_one)
-    send_partials(j_three, 1, part_three, got_three)
+    share_second(1)
+    share_first(2)
+    share_second(0)
     move(1)
-    share_grad(2)
-    emb_out[...] = take_partials(j_three, 1, got_three).astype(BF16)
     move(0)
+    share_second(2)
     take_move(1, three_out)
+    take_move(0, two_out)
+    emb_out[...] = take_partials(j_three, 1, got_three, 0, seeds).astype(BF16)
     one_out[...] = summed(2)
-    take_move(0, two_out)
 
     for leave in pending:
         leave()
@@ -478,6 +521,7 @@
     chunks_one, chunks_two = 4, 2
     dma = pltpu.SemaphoreType.DMA
     chips = groups // 2
+    side = math.isqrt(chips)
     scratch = [pltpu.VMEM((rows, SLOT), jnp.int32) for rows in (outer, mid, seeds)]
     scratch += [
         pltpu.VMEM((groups * SLOT, lanes), F32),
@@ -507,12 +551,14 @@
     ]
     scratch += [pltpu.VMEM((3, mid, width), BF16)] * 2 + [pltpu.VMEM((3, seeds, width), BF16)] * 2
     scratch += [pltpu.VMEM((3, groups, height, width), F32)]
-    scratch += [pltpu.VMEM((3, chips, height, width), BF16)] * 4
-    scratch += [pltpu.VMEM((2, height, width), F32)] * 2
+    scratch += [pltpu.VMEM((3, chips, height, width), BF16)] * 2
+    scratch += [pltpu.VMEM((3, 2, side, side, height // 2, width), BF16)] * 2
+    scratch += [pltpu.VMEM((3, 2, side, height // 2, width), kind) for kind in (F32, BF16, BF16)]
+    scratch += [pltpu.VMEM((2, height, width), BF16)] * 2
     scratch += [dma((4 + 2 * stores,)), dma((stores,)), dma((stores,))]
     scratch += [dma((3, chunks)) for chunks in (chunks_one, chunks_one, chunks_two, chunks_two)]
-    scratch += [dma((3,))] * 2 + [dma((2, 3))] * 2 + [dma((2,))] * 4 + [dma((2, 3))] * 2
-    scratch += [dma((3,))] * 4 + [dma((2,))] * 2
+    scratch += [dma((3,))] * 2 + [dma((2, 3))] * 2 + [dma((2,))] * 4 + [dma((2, chunks_two, 3))] * 2
+    scratch += [dma((3,))] * 2 + [dma((3, 2, side))] * 4 + [dma((2,))] * 2
     shapes = (
         jax.ShapeDtypeStruct((seeds, width), BF16),
         jax.ShapeDtypeStruct((height, width), F32),

time: 115 us -> 109 us (0.948)
  the two profiles are of different devices: /device:TPU:14 before, /device:TPU:3 now
where the time goes in v4:
time: 109 us; the launch traced here: 108 us
  Pallas kernels  107 us (98%)
    pallas_call x1, Pallas kernels, run(): pl.pallas_call(functools.partial(kernel, stores, groups, slots), out_shap...  106 us

profile of v4, /device:TPU:3, one launch (start us, length us, event | category | flops | bytes accessed | tf_op | source)
XLA Modules:
  0.0 108.1 jit_solution(10967818960699307640)
XLA Ops:
  0.6 105.8 %shard_map.165 = (bf16[192,256]{1,0:T(8,128)(2,1)}, f32[64,256]{1,0:T(8,128)}, f32[64,256]{1,0:T(8,128)}, f32[64,256]{1,0:T(8,128)}) custom-call(s32[12,1,32]{2,1,0:T(1,128)} %bitcast.7, s32[1,32]{1,0:T(1,128)} %sizes.1, s32[768]{0:T(1024)} %self_ids.1, s32[10,768]{1,0:T(8,128)} %bitcast.4, s32[768]{0:T(1024)} %degree_one.1, s32[10,384]{1,0:T(8,128)} %bitcast.5, ...), custom_call_target="tpu_custom_call" | custom-call | tf_op jit(solution)/shard_map/pallas_call | solution.py:568
  106.4 1.7 %shard_map.166 = (bf16[192,256]{1,0:T(8,128)(2,1)}, f32[64,256]{1,0:T(8,128)}, f32[64,256]{1,0:T(8,128)}, f32[64,256]{1,0:T(8,128)}) custom-call(bf16[192,256]{1,0:T(8,128)(2,1)} %get-tuple-element.8.refs_0_, f32[64,256]{1,0:T(8,128)} %get-tuple-element.9.refs_1_, f32[64,256]{1,0:T(8,128)} %get-tuple-element.10.refs_2_, f32[64,256]{1,0:T(8,128)} %get-tuple-element.11.refs_3_), custom_call_target="tpu_custom_call" | custom-call | tf_op jit(solution)/shard_map/pallas_call | solution.py:582

commit v5 on v4

--- a/solution.py
+++ b/solution.py
@@ -34,18 +34,21 @@
     return size
 
 
-def count_matches(ids, column_list, dst, rows, width):
-    high = step_of(rows, 16)
-    wide = step_of(width, 1024)
+def count_matches(ids, wanted, rows, width):
+    high = step_of(rows, 128)
+    wide = step_of(width, 256)
 
     def body(index, carry):
-        part = ids[rows_at(index, high), :]
+        here = rows_at(index, high)
+        part = ids[here, :].astype(jnp.int16)
         for start in range(0, width, wide):
-            place = lax.broadcasted_iota(jnp.int32, (high, wide), 1) + start
-            total = jnp.zeros((high, wide), F32)
-            for column in column_list:
-                total = total + jnp.where(part[:, column : column + 1] == place, 1.0, 0.0)
-            dst[rows_at(index, high), start : start + wide] = total.astype(BF16)
+            place = (lax.broadcasted_iota(jnp.int32, (high, wide), 1) + start).astype(jnp.int16)
+            for column_list, dst in wanted:
+                total = None
+                for column in column_list:
+                    found = jnp.where(part[:, column : column + 1] == place, BF16(1), BF16(0))
+                    total = found if total is None else total + found
+                dst[here, start : start + wide] = total
         return carry
 
     lax.fori_loop(0, rows // high, body, 0)
@@ -56,12 +59,12 @@
     sent, sizes, self_ids, near_one_t, degree_one, near_two_t, degree_two, near_three_t, degree_three,
     cot, feat_hbm, one_hbm, two_hbm, three_hbm,
     emb_out, one_out, two_out, three_out,
-    near_one, near_two, near_three, extra, feat, hot, picked, arrived, filled,
+    near_one, near_two, near_three, asked, extra, feat, hot, picked, landed, dense, inputs, fills, filled, valid, sums,
     tile_one, tile_self, tile_two, tile_three, w_one, w_rows,
     j_one, j_two, j_three, pre_one, pre_two, hid_one, hid_two, cots, dpres, spread_two, below3, dpre_one,
     part_two, got_two, part_three, got_three,
     full, px_send, px_recv, blk, rr, line, thin, last, move_send, move_recv,
-    load_sem, in_send, in_recv, ag1_send, ag1_recv, agd_send, agd_recv,
+    load_sem, in_send, in_recv, cn_ssem, cn_rsem, ag1_send, ag1_recv, agd_send, agd_recv,
     cot_ssem, cot_rsem, wz_ssem, wz_rsem, wp_ssem, wp_rsem, ws_ssem, ws_rsem,
     rs_ssem, rs_rsem, px_ssem, px_rsem, rr_ssem, rr_rsem, ls_ssem, ls_rsem, mv_ssem, mv_rsem,
 ):
@@ -76,7 +79,8 @@
     others = ((across, 2), (right, 0), (left, 1))
     width = cot.shape[1]
     seeds, mid, outer = cot.shape[0], near_two.shape[0], near_one.shape[0]
-    cells = devices * SLOT
+    kept = groups * slots
+    cells = stores * kept
     fan = near_two_t.shape[0]
     pending = []
 
@@ -126,13 +130,11 @@
     wanted = jnp.concatenate([sent[index] for index in range(slots)] + [jnp.full((SLOT - slots, groups), -1, jnp.int32)], axis=0)
     wanted = jnp.where(slot < amounts, wanted, -1)
     notes = jnp.where(slot == slots, amounts, 0).astype(F32)
-    wide = step_of(feat.shape[0], 1024)
     for group in range(groups):
         here = pl.ds(group * SLOT, SLOT)
         extra[here, :] = jnp.broadcast_to(notes[:, group : group + 1], (SLOT, extra.shape[1]))
-        for start in range(0, feat.shape[0], wide):
-            place = lax.broadcasted_iota(jnp.int32, (SLOT, wide), 1) + start
-            hot[here, start : start + wide] = jnp.where(wanted[:, group : group + 1] == place, 1.0, 0.0).astype(BF16)
+        asked[here, :] = jnp.broadcast_to(wanted[:, group : group + 1], (SLOT, SLOT))
+    count_matches(asked, [([0], hot)], groups * SLOT, feat.shape[0])
     loads[0].wait()
     pl.semaphore_wait(barrier, devices - 1)
 
@@ -144,48 +146,83 @@
             remote(piece_of(hbm, store), spot, wz_ssem.at[number, place], wz_rsem.at[number, place], store, t).start()
             pending.append(lambda number=number, place=place, spot=spot: await_bytes(spot, wz_ssem.at[number, place]))
 
-    def fetch(index, carry):
-        store = lax.rem(z + index, stores)
-        columns = pl.ds(pl.multiple_of(store * width, width), width)
+    def fetch(quarter, carry):
+        columns = pl.ds(pl.multiple_of(quarter * width, width), width)
         rows = step_of(groups * SLOT, 256)
         for start in range(0, groups * SLOT, rows):
             part = dot(hot[start : start + rows, :], feat[:, columns])
             counts = jnp.concatenate([extra[start : start + rows, :]] * (width // extra.shape[1]), axis=1)
-            picked[store, start : start + rows, :] = (part + counts).astype(BF16)
+            picked[quarter, start : start + rows, :] = (part + counts).astype(BF16)
 
         def send(number, inner):
             trainer = lax.rem(t + number * 13, groups)
-
-            @pl.when(jnp.logical_or(store != z, trainer != t))
-            def _():
-                remote(
-                    picked.at[store, rows_at(trainer, SLOT), :], arrived.at[rows_at(me, SLOT), :],
-                    in_send.at[store], in_recv.at[z], store, trainer,
-                ).start()
-
+            remote(
+                picked.at[quarter, rows_at(trainer, SLOT), :], landed.at[quarter, rows_at(t, SLOT), :],
+                in_send.at[quarter], in_recv.at[quarter], z, trainer,
+            ).start()
             return inner
 
-        lax.fori_loop(0, groups, send, 0)
+        lax.fori_loop(1, groups, send, 0)
+        pltpu.make_async_copy(
+            picked.at[quarter, rows_at(t, SLOT), :], landed.at[quarter, rows_at(t, SLOT), :], in_recv.at[quarter]
+        ).start()
         return carry
 
     lax.fori_loop(0, stores, fetch, 0)
-    own_block = pltpu.make_async_copy(
-        picked.at[z, rows_at(t, SLOT), :], arrived.at[rows_at(me, SLOT), :], in_recv.at[z]
-    )
-    own_block.start()
 
     def leave_blocks():
-        for index in range(stores):
-            store = lax.rem(z + index, stores)
-            amount = groups - (1 if index == 0 else 0)
-            await_bytes(picked.at[store, pl.ds(0, amount * SLOT), :], in_send.at[store])
+        for quarter in range(stores):
+            await_bytes(picked.at[quarter, pl.ds(0, (groups - 1) * SLOT), :], in_send.at[quarter])
 
     pending.append(leave_blocks)
+
+    def moved(index):
+        return index + (SLOT - slots) * ((index * ((1 << 19) // slots + 1)) >> 19)
+
+    from_row = moved(lax.broadcasted_iota(jnp.int32, (kept, 1), 0))
+    place = lax.broadcasted_iota(jnp.int32, (kept, groups * SLOT), 1)
+    dense[...] = jnp.where(from_row == place, 1.0, 0.0).astype(BF16)
+    ring_one = lambda source, index: inputs.at[index, pl.ds(pl.multiple_of(source * kept, kept), kept), :]
+
+    def start_gather(piece_at, index, send_sem, recv_sem):
+        piece = piece_at(z, index)
+        remote(piece, piece, send_sem.at[0, index], recv_sem.at[0, index], right, t).start()
+        remote(piece, piece, send_sem.at[1, index], recv_sem.at[1, index], left, t).start()
+
+    def take_gather(piece_at, chunks, send_sem, recv_sem, near, far, between):
+        for index in range(chunks):
+            for side_at, (source, onward) in enumerate(((left, right), (right, left))):
+                piece = piece_at(source, index)
+                await_bytes(piece, recv_sem.at[side_at, index])
+                if index % 2 == side_at:
+                    remote(piece, piece, send_sem.at[2, index], recv_sem.at[2, index], onward, t).start()
+            near(index)
+        between()
+        for index in range(chunks):
+            await_bytes(piece_at(across, index), recv_sem.at[2, index])
+            far(index)
+        for way in range(3):
+            for index in range(chunks):
+                pending.append(
+                    lambda way=way, index=index: await_bytes(piece_at(z, index), send_sem.at[way, index])
+                )
+
+    def pass_inputs(quarter):
+        await_bytes(landed.at[quarter], in_recv.at[quarter])
+        inputs[quarter, pl.ds(pl.multiple_of(z * kept, kept), kept), :] = dot(dense[...], landed[quarter]).astype(BF16)
+        start_gather(ring_one, quarter, ag1_send, ag1_recv)
+
+    pass_inputs(0)
+    owner = lax.broadcasted_iota(jnp.int32, (groups, 1), 0)
+    place = lax.broadcasted_iota(jnp.int32, (groups, groups * SLOT), 1)
+    note = jnp.where(owner * SLOT + slots == place, 1.0, 0.0).astype(BF16)
+    fills[z] = dot(note, landed[0, :, 0 : fills.shape[2]]).astype(BF16)
+    for store, place in others:
+        remote(fills.at[z], fills.at[z], cn_ssem.at[place], cn_rsem.at[place], store, t).start()
+        pending.append(lambda place=place: await_bytes(fills.at[z], cn_ssem.at[place]))
+    pass_inputs(1)
     for load in loads[1:]:
         load.wait()
-
-    def moved(index):
-        return index + (SLOT - slots) * ((index * ((1 << 19) // slots + 1)) >> 19)
 
     def upright(near, degree, own, dst):
         rows = near.shape[1]
@@ -194,13 +231,15 @@
         parts.append(jnp.full((SLOT - fan - len(own), rows), -1, jnp.int32))
         dst[...] = jnp.concatenate(parts, axis=0).T
 
-    upright(moved(near_one_t[...]), degree_one, [moved(self_ids[...][None, :])], near_one)
+    upright(near_one_t[...], degree_one, [self_ids[...][None, :]], near_one)
     upright(near_two_t[...], degree_two, [], near_two)
     upright(near_three_t[...], degree_three, [], near_three)
-    count_matches(near_one, list(range(fan)), tile_one, outer, cells)
-    count_matches(near_one, [fan], tile_self, outer, cells)
-    count_matches(near_two, list(range(fan)), tile_two, mid, outer)
-    count_matches(near_three, list(range(fan)), tile_three, seeds, mid)
+    slots_used = list(range(fan))
+    count_matches(near_one, [(slots_used, tile_one), ([fan], tile_self)], outer, cells)
+    count_matches(near_two, [(slots_used, tile_two)], mid, outer)
+    count_matches(near_three, [(slots_used, tile_three)], seeds, mid)
+    for quarter in range(2, stores):
+        pass_inputs(quarter)
 
     def counted(near):
         return 1.0 + jnp.sum(jnp.where(near[...] >= 0, 1.0, 0.0), axis=1, keepdims=True)
@@ -212,61 +251,6 @@
         upper = below[:rows] + (total[:, :width] + scaled.astype(F32))
         return jnp.concatenate([upper, below[rows:]], axis=0)
 
-    def start_gather(held, index, rows, send_sem, recv_sem):
-        piece = held.at[z, rows_at(index, rows), :]
-        remote(piece, piece, send_sem.at[0, index], recv_sem.at[0, index], right, t).start()
-        remote(piece, piece, send_sem.at[1, index], recv_sem.at[1, index], left, t).start()
-
-    def take_gather(held, chunks, rows, send_sem, recv_sem, use, between):
-        for index in range(chunks):
-            here = rows_at(index, rows)
-            for side, (source, onward) in enumerate(((left, right), (right, left))):
-                piece = held.at[source, here, :]
-                await_bytes(piece, recv_sem.at[side, index])
-                if index % 2 == side:
-                    remote(piece, piece, send_sem.at[2, index], recv_sem.at[2, index], onward, t).start()
-            for source in (left, right):
-                use(source, here)
-        between()
-        for index in range(chunks):
-            here = rows_at(index, rows)
-            await_bytes(held.at[across, here, :], recv_sem.at[2, index])
-            use(across, here)
-        for way in range(3):
-            for index in range(chunks):
-                pending.append(
-                    lambda way=way, here=rows_at(index, rows), index=index: await_bytes(
-                        held.at[z, here, :], send_sem.at[way, index]
-                    )
-                )
-
-    def mark(index, carry):
-        here = rows_at(index, SLOT)
-        block = arrived[here, 0 : filled.shape[1]].astype(F32)
-        place = lax.broadcasted_iota(jnp.int32, block.shape, 0).astype(F32)
-        filled[here, :] = jnp.where(place < block[slots : slots + 1, :], 1.0, 0.0).astype(BF16)
-        return carry
-
-    for store in range(stores):
-        await_bytes(arrived.at[pl.ds(store * groups * SLOT, groups * SLOT), :], in_recv.at[store])
-        lax.fori_loop(store * groups, (store + 1) * groups, mark, 0)
-
-    chunks_one = ag1_send.shape[1]
-    rows_one = outer // chunks_one
-
-    def layer_one(index, carry):
-        here = rows_at(index, rows_one)
-        own = dot(tile_self[here, :], arrived[...])
-        valid = 1.0 + dot(tile_one[here, :], filled[...])
-        valid = jnp.concatenate([valid] * (width // valid.shape[1]), axis=1)
-        mean = (own + dot(tile_one[here, :], arrived[...])) / valid
-        j_one[z, here, :] = jnp.concatenate([own, mean], axis=1).astype(BF16)
-        start_gather(j_one, index, rows_one, ag1_send, ag1_recv)
-        pre_one[here, :] = dot(j_one[z, here, :], w_one[z])
-        return carry
-
-    lax.fori_loop(0, chunks_one, layer_one, 0)
-
     for number in range(2):
         for store, place in others:
             await_bytes(w_rows.at[number, core, chip, store], wz_rsem.at[number, place])
@@ -280,8 +264,50 @@
         lax.fori_loop(1, chips, pass_on, 0)
         pending.append(lambda number=number: await_bytes(w_rows.at[number, core, pl.ds(0, chips - 1)], wp_ssem.at[number]))
 
-    def use_one(source, here):
-        pre_one[here, :] += dot(j_one[source, here, :], w_one[source])
+    def note_filled():
+        for store, place in others:
+            await_bytes(fills.at[store], cn_rsem.at[place])
+        row = lax.broadcasted_iota(jnp.int32, (kept, 1), 0)
+        owner = (row * ((1 << 19) // slots + 1)) >> 19
+        place = lax.broadcasted_iota(jnp.int32, (kept, groups), 1)
+        pick = jnp.where(owner == place, 1.0, 0.0).astype(BF16)
+        spot = (row - owner * slots).astype(F32)
+        for store in range(stores):
+            amount = dot(pick, fills[store])
+            filled[store * kept : (store + 1) * kept, :] = jnp.where(spot < amount, 1.0, 0.0).astype(BF16)
+        valid[...] = 1.0 + dot(tile_one[...], filled[...])
+
+    rows_one = outer // 2
+
+    def plane_part(tile, here, quarter, store):
+        spot = pl.ds(pl.multiple_of(store * kept, kept), kept)
+        return dot(tile[here, spot], inputs[quarter, spot, :])
+
+    def start_sums(quarter):
+        def body(index, carry):
+            here = rows_at(index, rows_one)
+            for place, tile in enumerate((tile_self, tile_one)):
+                sums[quarter, place, here, :] = (
+                    plane_part(tile, here, quarter, z)
+                    + plane_part(tile, here, quarter, left)
+                    + plane_part(tile, here, quarter, right)
+                )
+            return carry
+
+        lax.fori_loop(0, 2, body, 0)
+
+    def layer_one(quarter):
+        def body(index, carry):
+            here = rows_at(index, rows_one)
+            own = sums[quarter, 0, here, :] + plane_part(tile_self, here, quarter, across)
+            total = own + (sums[quarter, 1, here, :] + plane_part(tile_one, here, quarter, across))
+            mean = total / jnp.concatenate([valid[here, :]] * (width // valid.shape[1]), axis=1)
+            j_one[quarter, here, :] = jnp.concatenate([own, mean], axis=1).astype(BF16)
+            part = dot(j_one[quarter, here, :], w_one[quarter])
+            pre_one[here, :] = part if quarter == 0 else pre_one[here, :] + part
+            return carry
+
+        lax.fori_loop(0, 2, body, 0)
 
     def swap_weights():
         for number in range(2):
@@ -290,7 +316,11 @@
             remote(spot, spot, ws_ssem.at[number], ws_rsem.at[number], z, sibling).start()
             pending.append(lambda spot=spot, number=number: await_bytes(spot, ws_ssem.at[number]))
 
-    take_gather(j_one, chunks_one, rows_one, ag1_send, ag1_recv, use_one, swap_weights)
+    def before_sums():
+        swap_weights()
+        note_filled()
+
+    take_gather(ring_one, stores, ag1_send, ag1_recv, start_sums, layer_one, before_sums)
     hid_one[...] = (pre_one[...] * jax.nn.sigmoid(pre_one[...])).astype(BF16)
     for number in range(2):
         await_bytes(w_rows.at[number, 1 - core], ws_rsem.at[number])
@@ -325,6 +355,7 @@
     join(hid_one, near_two, tile_two, j_two)
     chunks_two = agd_send.shape[1]
     rows_two = mid // chunks_two
+    ring_two = lambda source, index: dpres.at[source, rows_at(index, rows_two), :]
     send_partials(j_two, 0, part_two, got_two, chunks_two)
     for store, place in others:
         await_bytes(cots.at[store], cot_rsem.at[place])
@@ -336,7 +367,7 @@
         here = rows_at(index, rows_two)
         pre_two[here, :] = take_partials(j_two, 0, got_two, index, rows_two)
         dpres[z, here, :] = (below3[here, :] * slope(pre_two[here, :])).astype(BF16)
-        start_gather(dpres, index, rows_two, agd_send, agd_recv)
+        start_gather(ring_two, index, agd_send, agd_recv)
     hid_two[...] = (pre_two[...] * jax.nn.sigmoid(pre_two[...])).astype(BF16)
     join(hid_two, near_three, tile_three, j_three)
 
@@ -469,12 +500,19 @@
         out[...] = move_recv[number].astype(F32)
 
     grad_of_rows(1, j_three, cots)
-    spread_two[...] = dot(dpres[z], rows_of(0, z), 1, 1)
-
-    def use_two(source, here):
-        spread_two[here, :] += dot(dpres[source, here, :], rows_of(0, source), 1, 1)
-
-    take_gather(dpres, chunks_two, rows_two, agd_send, agd_recv, use_two, lambda: share_first(1))
+
+    def spread_part(here, source):
+        return dot(dpres[source, here, :], rows_of(0, source), 1, 1)
+
+    def near_two_spread(index):
+        here = rows_at(index, rows_two)
+        spread_two[here, :] = spread_part(here, z) + spread_part(here, left) + spread_part(here, right)
+
+    def far_two_spread(index):
+        here = rows_at(index, rows_two)
+        spread_two[here, :] += spread_part(here, across)
+
+    take_gather(ring_two, chunks_two, agd_send, agd_recv, near_two_spread, far_two_spread, lambda: share_first(1))
     send_partials(j_three, 1, part_three, got_three, 1)
     grad_of_rows(0, j_two, dpres)
     below2 = spread_below(spread_two[...], near_two, tile_two)
@@ -512,24 +550,29 @@
     fwidth = features.shape[1]
     width = cotangent.shape[1]
     devices = stores * groups
-    cells = devices * SLOT
+    cells = devices * slots
     height = 2 * fwidth // groups
 
     vmem = pl.BlockSpec(memory_space=pltpu.VMEM)
     hbm = pl.BlockSpec(memory_space=pl.ANY)
     lanes = min(128, width)
-    chunks_one, chunks_two = 4, 2
+    chunks_two = 2
     dma = pltpu.SemaphoreType.DMA
     chips = groups // 2
     side = math.isqrt(chips)
-    scratch = [pltpu.VMEM((rows, SLOT), jnp.int32) for rows in (outer, mid, seeds)]
+    scratch = [pltpu.VMEM((rows, SLOT), jnp.int32) for rows in (outer, mid, seeds, groups * SLOT)]
     scratch += [
         pltpu.VMEM((groups * SLOT, lanes), F32),
         pltpu.VMEM(features.shape, BF16),
         pltpu.VMEM((groups * SLOT, features.shape[0]), BF16),
         pltpu.VMEM((stores, groups * SLOT, width), BF16),
-        pltpu.VMEM((cells, width), BF16),
+        pltpu.VMEM((stores, groups * SLOT, width), BF16),
+        pltpu.VMEM((groups * slots, groups * SLOT), BF16),
+        pltpu.VMEM((stores, cells, width), BF16),
+        pltpu.VMEM((stores, groups, lanes), BF16),
         pltpu.VMEM((cells, lanes), BF16),
+        pltpu.VMEM((outer, lanes), F32),
+        pltpu.VMEM((stores, 2, outer, width), F32),
         pltpu.VMEM((outer, cells), BF16),
         pltpu.VMEM((outer, cells), BF16),
         pltpu.VMEM((mid, outer), BF16),
@@ -555,8 +598,8 @@
     scratch += [pltpu.VMEM((3, 2, side, side, height // 2, width), BF16)] * 2
     scratch += [pltpu.VMEM((3, 2, side, height // 2, width), kind) for kind in (F32, BF16, BF16)]
     scratch += [pltpu.VMEM((2, height, width), BF16)] * 2
-    scratch += [dma((4 + 2 * stores,)), dma((stores,)), dma((stores,))]
-    scratch += [dma((3, chunks)) for chunks in (chunks_one, chunks_one, chunks_two, chunks_two)]
+    scratch += [dma((4 + 2 * stores,)), dma((stores,)), dma((stores,)), dma((3,)), dma((3,))]
+    scratch += [dma((3, chunks)) for chunks in (stores, stores, chunks_two, chunks_two)]
     scratch += [dma((3,))] * 2 + [dma((2, 3))] * 2 + [dma((2,))] * 4 + [dma((2, chunks_two, 3))] * 2
     scratch += [dma((3,))] * 2 + [dma((3, 2, side))] * 4 + [dma((2,))] * 2
     shapes = (

time: 109 us -> 93.5 us (0.86)
  Pallas kernels: 107 us -> 92.2 us
    pallas_call x1, Pallas kernels: 106 us -> 90.5 us  [run(): pl.pallas_call(functools.partial(kernel, stores, groups, slots), out_shap...]
where the time goes in v5:
time: 93.5 us; the launch traced here: 92.8 us
  Pallas kernels  92.2 us (99%)
    pallas_call x1, Pallas kernels, run(): pl.pallas_call(functools.partial(kernel, stores, groups, slots), out_shap...  90.5 us

profile of v5, /device:TPU:3, one launch (start us, length us, event | category | flops | bytes accessed | tf_op | source)
XLA Modules:
  0.0 92.8 jit_solution(7147890996782948303)
XLA Ops:
  0.6 90.5 %shard_map.165 = (bf16[192,256]{1,0:T(8,128)(2,1)}, f32[64,256]{1,0:T(8,128)}, f32[64,256]{1,0:T(8,128)}, f32[64,256]{1,0:T(8,128)}) custom-call(s32[12,1,32]{2,1,0:T(1,128)} %bitcast.7, s32[1,32]{1,0:T(1,128)} %sizes.1, s32[768]{0:T(1024)} %self_ids.1, s32[10,768]{1,0:T(8,128)} %bitcast.4, s32[768]{0:T(1024)} %degree_one.1, s32[10,384]{1,0:T(8,128)} %bitcast.5, ...), custom_call_target="tpu_custom_call" | custom-call | tf_op jit(solution)/shard_map/pallas_call | solution.py:611
  91.2 1.7 %shard_map.166 = (bf16[192,256]{1,0:T(8,128)(2,1)}, f32[64,256]{1,0:T(8,128)}, f32[64,256]{1,0:T(8,128)}, f32[64,256]{1,0:T(8,128)}) custom-call(bf16[192,256]{1,0:T(8,128)(2,1)} %get-tuple-element.8.refs_0_, f32[64,256]{1,0:T(8,128)} %get-tuple-element.9.refs_1_, f32[64,256]{1,0:T(8,128)} %get-tuple-element.10.refs_2_, f32[64,256]{1,0:T(8,128)} %get-tuple-element.11.refs_3_), custom_call_target="tpu_custom_call" | custom-call | tf_op jit(solution)/shard_map/pallas_call | solution.py:625

commit v6 on v5

--- a/solution.py
+++ b/solution.py
@@ -374,16 +374,16 @@
     height = full.shape[2]
     per_slice = width // height
 
-    def pack(number):
-        def body(index, carry):
-            px_send[number, index] = full[number, index * 2 + 1 - core].astype(BF16)
-            return carry
-
-        lax.fori_loop(0, chips, body, 0)
+    def pass_over(number, first, amount):
+        spot = pl.ds(first, amount)
         remote(
-            px_send.at[number], px_recv.at[number], px_ssem.at[number], px_rsem.at[number], z, sibling
+            px_send.at[number, spot], px_recv.at[number, spot], px_ssem.at[number], px_rsem.at[number], z, sibling
         ).start()
+
+    def left_over(number):
         pending.append(lambda: await_bytes(px_send.at[number], px_ssem.at[number]))
+
+    pairs = per_slice // 2 if per_slice % 2 == 0 else 0
 
     def grad_of_columns(number, joined, dpre):
         def products(store, carry):
@@ -392,20 +392,45 @@
                 for index in range(per_slice):
                     start = half * width + index * height
                     full[number, half * (groups // 2) + store * per_slice + index] = part[start : start + height, :]
+            for half in range(2):
+                for index in range(pairs):
+                    block = half * (groups // 2) + store * per_slice + 2 * index + 1 - core
+                    px_send[number, store * per_slice + half * pairs + index] = full[number, block].astype(BF16)
+            if pairs:
+                pass_over(number, store * per_slice, per_slice)
             return carry
 
         lax.fori_loop(0, stores, products, 0)
-        pack(number)
-
-    def grad_of_rows(number, joined, columns):
-        def products(store, carry):
-            part = dot(joined[...], columns[store], 0, 0)
+        if not pairs:
+            for index in range(chips):
+                px_send[number, index] = full[number, index * 2 + 1 - core].astype(BF16)
+            pass_over(number, 0, chips)
+        left_over(number)
+
+    def column_slot(index):
+        if not pairs:
+            return index
+        half, rest = index // (chips // 2), lax.rem(index, chips // 2)
+        return rest // pairs * per_slice + half * pairs + lax.rem(rest, pairs)
+
+    def grad_of_rows(number, joined, columns, store):
+        part = dot(joined[...], columns[store], 0, 0)
+        passed = lax.rem(store, 2) != core
+        first = store // 2 * 2 * per_slice
+
+        @pl.when(passed)
+        def _():
+            for index in range(2 * per_slice):
+                px_send[number, first + index] = part[index * height : (index + 1) * height, :].astype(BF16)
+            pass_over(number, first, 2 * per_slice)
+
+        @pl.when(jnp.logical_not(passed))
+        def _():
             for index in range(2 * per_slice):
                 full[number, index * stores + store] = part[index * height : (index + 1) * height, :]
-            return carry
-
-        lax.fori_loop(0, stores, products, 0)
-        pack(number)
+
+    def row_slot(index):
+        return lax.rem(index, stores // 2) * 2 * per_slice + index // (stores // 2)
 
     side = rr.shape[2]
     place_x, place_y = chip // side, lax.rem(chip, side)
@@ -416,11 +441,11 @@
         column = (target, place_y) if way == 0 else (place_x, target)
         return target, (column[0] * side + column[1]) * 2 + core
 
-    def share_first(number):
+    def share_first(number, slot_of):
         await_bytes(px_recv.at[number], px_rsem.at[number])
 
         def body(index, carry):
-            total = full[number, index * 2 + core] + px_recv[number, index].astype(F32)
+            total = full[number, index * 2 + core] + px_recv[number, slot_of(index)].astype(F32)
             first, second = index // side, lax.rem(index, side)
             blk[number, 0, first, second] = total[: height // 2].astype(BF16)
             blk[number, 1, second, first] = total[height // 2 :].astype(BF16)
@@ -499,7 +524,9 @@
         await_bytes(move_recv.at[number], mv_rsem.at[number])
         out[...] = move_recv[number].astype(F32)
 
-    grad_of_rows(1, j_three, cots)
+    for turn in range(stores):
+        grad_of_rows(1, j_three, cots, lax.rem(core + 1 + turn * 2 + turn // 2, stores))
+    left_over(1)
 
     def spread_part(here, source):
         return dot(dpres[source, here, :], rows_of(0, source), 1, 1)
@@ -512,15 +539,21 @@
         here = rows_at(index, rows_two)
         spread_two[here, :] += spread_part(here, across)
 
-    take_gather(ring_two, chunks_two, agd_send, agd_recv, near_two_spread, far_two_spread, lambda: share_first(1))
-    send_partials(j_three, 1, part_three, got_three, 1)
-    grad_of_rows(0, j_two, dpres)
+    def meanwhile():
+        share_first(1, row_slot)
+        for store in (left, right, z):
+            grad_of_rows(0, j_two, dpres, store)
+
+    take_gather(ring_two, chunks_two, agd_send, agd_recv, near_two_spread, far_two_spread, meanwhile)
+    grad_of_rows(0, j_two, dpres, across)
+    left_over(0)
     below2 = spread_below(spread_two[...], near_two, tile_two)
     dpre_one[...] = (below2 * slope(pre_one[...])).astype(BF16)
-    share_first(0)
+    share_first(0, row_slot)
     grad_of_columns(2, j_one, dpre_one)
     share_second(1)
-    share_first(2)
+    send_partials(j_three, 1, part_three, got_three, 1)
+    share_first(2, column_slot)
     share_second(0)
     move(1)
     move(0)
@@ -556,7 +589,7 @@
     vmem = pl.BlockSpec(memory_space=pltpu.VMEM)
     hbm = pl.BlockSpec(memory_space=pl.ANY)
     lanes = min(128, width)
-    chunks_two = 2
+    chunks_two = 4
     dma = pltpu.SemaphoreType.DMA
     chips = groups // 2
     side = math.isqrt(chips)

time: 93.5 us -> 90.3 us (0.966)
  Pallas kernels: 92.2 us -> 89.5 us
    pallas_call x1, Pallas kernels: 90.5 us -> 87.8 us  [run(): pl.pallas_call(functools.partial(kernel, stores, groups, slots), out_shap...]
where the time goes in v6:
time: 90.3 us; the launch traced here: 90.1 us
  Pallas kernels  89.5 us (99%)
    pallas_call x1, Pallas kernels, run(): pl.pallas_call(functools.partial(kernel, stores, groups, slots), out_shap...  87.8 us

profile of v6, /device:TPU:3, one launch (start us, length us, event | category | flops | bytes accessed | tf_op | source)
XLA Modules:
  0.0 90.1 jit_solution(2444032855419765058)
XLA Ops:
  0.6 87.8 %shard_map.165 = (bf16[192,256]{1,0:T(8,128)(2,1)}, f32[64,256]{1,0:T(8,128)}, f32[64,256]{1,0:T(8,128)}, f32[64,256]{1,0:T(8,128)}) custom-call(s32[12,1,32]{2,1,0:T(1,128)} %bitcast.7, s32[1,32]{1,0:T(1,128)} %sizes.1, s32[768]{0:T(1024)} %self_ids.1, s32[10,768]{1,0:T(8,128)} %bitcast.4, s32[768]{0:T(1024)} %degree_one.1, s32[10,384]{1,0:T(8,128)} %bitcast.5, ...), custom_call_target="tpu_custom_call" | custom-call | tf_op jit(solution)/shard_map/pallas_call | solution.py:644
  88.5 1.7 %shard_map.166 = (bf16[192,256]{1,0:T(8,128)(2,1)}, f32[64,256]{1,0:T(8,128)}, f32[64,256]{1,0:T(8,128)}, f32[64,256]{1,0:T(8,128)}) custom-call(bf16[192,256]{1,0:T(8,128)(2,1)} %get-tuple-element.8.refs_0_, f32[64,256]{1,0:T(8,128)} %get-tuple-element.9.refs_1_, f32[64,256]{1,0:T(8,128)} %get-tuple-element.10.refs_2_, f32[64,256]{1,0:T(8,128)} %get-tuple-element.11.refs_3_), custom_call_target="tpu_custom_call" | custom-call | tf_op jit(solution)/shard_map/pallas_call | solution.py:658

commit v7 on v6

--- a/solution.py
+++ b/solution.py
@@ -344,28 +344,57 @@
                 remote(part.at[place, here, :], got.at[place, here, :], *sems, store, t).start()
                 pending.append(lambda place=place, here=here, sem=sems[0]: await_bytes(part.at[place, here, :], sem))
 
-    def take_partials(joined, number, got, index, rows):
+    def take_partials(joined, number, got, index, rows, places):
         here = pl.ds(index * rows, rows)
         total = dot(joined[here, :], rows_of(number, z))
-        for place in range(3):
+        for place in range(places):
             await_bytes(got.at[place, here, :], rs_rsem.at[number, index, place])
             total = total + got[place, here, :].astype(F32)
         return total
+
+    def send_by(index, place, store):
+        here = pl.ds(index * rows_two, rows_two)
+        sems = rs_ssem.at[0, index, place], rs_rsem.at[0, index, place]
+        remote(part_two.at[place, here, :], got_two.at[place, here, :], *sems, store, t).start()
+        pending.append(lambda: await_bytes(part_two.at[place, here, :], sems[0]))
+
+    def start_ring():
+        for index in range(chunks_two):
+            here = pl.ds(index * rows_two, rows_two)
+            part_two[2, here, :] = dot(j_two[here, :], rows_of(0, across)).astype(BF16)
+            send_by(index, 2, (right, left)[index % 2])
+        for index in range(chunks_two):
+            here = pl.ds(index * rows_two, rows_two)
+            place = 1 - index % 2
+            store = (right, left)[place]
+            part_two[place, here, :] = dot(j_two[here, :], rows_of(0, store)).astype(BF16)
+            send_by(index, place, store)
+
+    def close_ring():
+        for index in range(chunks_two):
+            here = pl.ds(index * rows_two, rows_two)
+            place = index % 2
+            store = (right, left)[place]
+            total = dot(j_two[here, :], rows_of(0, store))
+            await_bytes(got_two.at[2, here, :], rs_rsem.at[0, index, 2])
+            part_two[place, here, :] = (total + got_two[2, here, :].astype(F32)).astype(BF16)
+            send_by(index, place, store)
 
     join(hid_one, near_two, tile_two, j_two)
     chunks_two = agd_send.shape[1]
     rows_two = mid // chunks_two
     ring_two = lambda source, index: dpres.at[source, rows_at(index, rows_two), :]
-    send_partials(j_two, 0, part_two, got_two, chunks_two)
+    start_ring()
     for store, place in others:
         await_bytes(cots.at[store], cot_rsem.at[place])
     spread = dot(cots[0], rows_of(1, 0), 1, 1)
     for store in range(1, stores):
         spread = spread + dot(cots[store], rows_of(1, store), 1, 1)
     below3[...] = spread_below(spread, near_three, tile_three)
+    close_ring()
     for index in range(chunks_two):
         here = rows_at(index, rows_two)
-        pre_two[here, :] = take_partials(j_two, 0, got_two, index, rows_two)
+        pre_two[here, :] = take_partials(j_two, 0, got_two, index, rows_two, 2)
         dpres[z, here, :] = (below3[here, :] * slope(pre_two[here, :])).astype(BF16)
         start_gather(ring_two, index, agd_send, agd_recv)
     hid_two[...] = (pre_two[...] * jax.nn.sigmoid(pre_two[...])).astype(BF16)
@@ -549,6 +578,8 @@
     left_over(0)
     below2 = spread_below(spread_two[...], near_two, tile_two)
     dpre_one[...] = (below2 * slope(pre_one[...])).astype(BF16)
+    early = list(pending)
+    pending.clear()
     share_first(0, row_slot)
     grad_of_columns(2, j_one, dpre_one)
     share_second(1)
@@ -557,10 +588,12 @@
     share_second(0)
     move(1)
     move(0)
+    for leave in early:
+        leave()
     share_second(2)
     take_move(1, three_out)
     take_move(0, two_out)
-    emb_out[...] = take_partials(j_three, 1, got_three, 0, seeds).astype(BF16)
+    emb_out[...] = take_partials(j_three, 1, got_three, 0, seeds, 3).astype(BF16)
     one_out[...] = summed(2)
 
     for leave in pending:

time: 90.3 us -> 89.4 us (0.990)
  no operation moved by 1% of the time
where the time goes in v7:
time: 89.4 us; the launch traced here: 89.2 us
  Pallas kernels  88.6 us (99%)
    pallas_call x1, Pallas kernels, run(): pl.pallas_call(functools.partial(kernel, stores, groups, slots), out_shap...  86.9 us

profile of v7, /device:TPU:3, one launch (start us, length us, event | category | flops | bytes accessed | tf_op | source)
XLA Modules:
  0.0 89.2 jit_solution(8653532927819066462)
XLA Ops:
  0.6 86.9 %shard_map.165 = (bf16[192,256]{1,0:T(8,128)(2,1)}, f32[64,256]{1,0:T(8,128)}, f32[64,256]{1,0:T(8,128)}, f32[64,256]{1,0:T(8,128)}) custom-call(s32[12,1,32]{2,1,0:T(1,128)} %bitcast.7, s32[1,32]{1,0:T(1,128)} %sizes.1, s32[768]{0:T(1024)} %self_ids.1, s32[10,768]{1,0:T(8,128)} %bitcast.4, s32[768]{0:T(1024)} %degree_one.1, s32[10,384]{1,0:T(8,128)} %bitcast.5, ...), custom_call_target="tpu_custom_call" | custom-call | tf_op jit(solution)/shard_map/pallas_call | solution.py:677
  87.6 1.7 %shard_map.166 = (bf16[192,256]{1,0:T(8,128)(2,1)}, f32[64,256]{1,0:T(8,128)}, f32[64,256]{1,0:T(8,128)}, f32[64,256]{1,0:T(8,128)}) custom-call(bf16[192,256]{1,0:T(8,128)(2,1)} %get-tuple-element.8.refs_0_, f32[64,256]{1,0:T(8,128)} %get-tuple-element.9.refs_1_, f32[64,256]{1,0:T(8,128)} %get-tuple-element.10.refs_2_, f32[64,256]{1,0:T(8,128)} %get-tuple-element.11.refs_3_), custom_call_target="tpu_custom_call" | custom-call | tf_op jit(solution)/shard_map/pallas_call | solution.py:691

commit v8 on v7

--- a/solution.py
+++ b/solution.py
@@ -591,10 +591,10 @@
     for leave in early:
         leave()
     share_second(2)
+    emb_out[...] = take_partials(j_three, 1, got_three, 0, seeds, 3).astype(BF16)
     take_move(1, three_out)
+    one_out[...] = summed(2)
     take_move(0, two_out)
-    emb_out[...] = take_partials(j_three, 1, got_three, 0, seeds, 3).astype(BF16)
-    one_out[...] = summed(2)
 
     for leave in pending:
         leave()

time: 89.4 us -> 89.1 us (level)
  no operation moved by 1% of the time
where the time goes in v8:
time: 89.1 us; the launch traced here: 88.9 us
  Pallas kernels  88.2 us (99%)
    pallas_call x1, Pallas kernels, run(): pl.pallas_call(functools.partial(kernel, stores, groups, slots), out_shap...  86.6 us

profile of v8, /device:TPU:3, one launch (start us, length us, event | category | flops | bytes accessed | tf_op | source)
XLA Modules:
  0.0 88.9 jit_solution(11638742887518759158)
XLA Ops:
  0.6 86.6 %shard_map.165 = (bf16[192,256]{1,0:T(8,128)(2,1)}, f32[64,256]{1,0:T(8,128)}, f32[64,256]{1,0:T(8,128)}, f32[64,256]{1,0:T(8,128)}) custom-call(s32[12,1,32]{2,1,0:T(1,128)} %bitcast.7, s32[1,32]{1,0:T(1,128)} %sizes.1, s32[768]{0:T(1024)} %self_ids.1, s32[10,768]{1,0:T(8,128)} %bitcast.4, s32[768]{0:T(1024)} %degree_one.1, s32[10,384]{1,0:T(8,128)} %bitcast.5, ...), custom_call_target="tpu_custom_call" | custom-call | tf_op jit(solution)/shard_map/pallas_call | solution.py:677
  87.2 1.7 %shard_map.166 = (bf16[192,256]{1,0:T(8,128)(2,1)}, f32[64,256]{1,0:T(8,128)}, f32[64,256]{1,0:T(8,128)}, f32[64,256]{1,0:T(8,128)}) custom-call(bf16[192,256]{1,0:T(8,128)(2,1)} %get-tuple-element.8.refs_0_, f32[64,256]{1,0:T(8,128)} %get-tuple-element.9.refs_1_, f32[64,256]{1,0:T(8,128)} %get-tuple-element.10.refs_2_, f32[64,256]{1,0:T(8,128)} %get-tuple-element.11.refs_3_), custom_call_target="tpu_custom_call" | custom-call | tf_op jit(solution)/shard_map/pallas_call | solution.py:691
